TPU v7x, 128 devices: a whole 4x4x4 slice. The times are simulated.
128 devices in a mesh: fsdp: 64 (over x, y_hi, z, core), rep: 2 (over y_lo).
Axes of the slice: x: 4, y: 4 (y_hi: 2, y_lo: 2; y = y_hi * 2 + y_lo), z: 4, core: 2. Of those that a mesh axis runs over, the one named last changes fastest.
Arguments:
- tokens: bfloat16 [2, 16384, 1152], P(None, ('fsdp', 'rep')), may hold values from -6 to 6
- picture: int32 [2, 16384], replicated, may hold values from -16384 to 319, as said below
- cotangent: bfloat16 [2, 16384, 1152], P(None, ('fsdp', 'rep')), may hold values from -6 to 6
- ln1_gain: float32 [1152], replicated, may hold values from 0.1 to 1.9
- ln1_bias: float32 [1152], replicated, may hold values from -1.75 to 1.75
- w_query: bfloat16 [1152, 1152], P('fsdp'), may hold values from -0.1875 to 0.1875
- b_query: float32 [1152], replicated, may hold values from -1.75 to 1.75
- w_key: bfloat16 [1152, 1152], P('fsdp'), may hold values from -0.1875 to 0.1875
- w_value: bfloat16 [1152, 1152], P('fsdp'), may hold values from -0.1875 to 0.1875
- b_value: float32 [1152], replicated, may hold values from -1.75 to 1.75
- w_out: bfloat16 [1152, 1152], P('fsdp'), may hold values from -0.875 to 0.875
- b_out: float32 [1152], replicated, may hold values from -1.75 to 1.75
- ln2_gain: float32 [1152], replicated, may hold values from 0.1 to 1.9
- ln2_bias: float32 [1152], replicated, may hold values from -1.75 to 1.75
- w_fc1: bfloat16 [1152, 4304], P('fsdp'), may hold values from -0.1875 to 0.1875
- b_fc1: float32 [4304], replicated, may hold values from -1.75 to 1.75
- w_fc2: bfloat16 [4304, 1152], P(None, 'fsdp'), may hold values from -0.09375 to 0.09375
- b_fc2: float32 [1152], replicated, may hold values from -1.75 to 1.75
Outputs:
- mixed: bfloat16 [2, 16384, 1152], P(None, ('fsdp', 'rep'))
- grad_tokens: bfloat16 [2, 16384, 1152], P(None, ('fsdp', 'rep'))
- grad_ln1_gain: float32 [1152], replicated
- grad_ln1_bias: float32 [1152], replicated
- grad_w_query: float32 [1152, 1152], P('fsdp')
- grad_b_query: float32 [1152], replicated
- grad_w_key: float32 [1152, 1152], P('fsdp')
- grad_w_value: float32 [1152, 1152], P('fsdp')
- grad_b_value: float32 [1152], replicated
- grad_w_out: float32 [1152, 1152], P('fsdp')
- grad_b_out: float32 [1152], replicated
- grad_ln2_gain: float32 [1152], replicated
- grad_ln2_bias: float32 [1152], replicated
- grad_w_fc1: float32 [1152, 4304], P('fsdp')
- grad_b_fc1: float32 [4304], replicated
- grad_w_fc2: float32 [4304, 1152], P(None, 'fsdp')
- grad_b_fc2: float32 [1152], replicated
Inputs may be any that keep to these rules, and one draw needn't show every extreme that they name: Tokens with one nonnegative id form one picture of 100 to 1024 consecutive tokens inside one packed row of 2048 tokens (rows are consecutive runs of 2048 tokens); each row begins with a picture of odd length followed by a picture of exactly 1024 tokens; every negative id marks a padding token and occurs once in its micro-batch.
All inputs are finite; a program needn't handle non-finite values.
Results may differ from a plain program's by a relative error of at most 0.014.
Values may be sent and summed in bfloat16 or wider, within the bound.
A program may use at most 320 MiB of HBM per device.

v0:
```python
import functools

import jax
import jax.numpy as jnp
import numpy as np
from jax import lax
from jax.experimental import pallas as pl
from jax.experimental.pallas import tpu as pltpu
from jax.sharding import PartitionSpec as P

MESH = pl.DeviceIdType.MESH
BF = jnp.bfloat16
F32 = jnp.float32
LANES = 128
ORDERS = (("x", "y", "z"), ("y", "z", "x"), ("z", "x", "y"))
AXES = ("x", "y", "z")


def here():
    shard = lax.axis_index("fsdp")
    low = lax.axis_index("rep")
    place = {
        "x": lax.div(shard, 16),
        "y": lax.rem(lax.div(shard, 8), 2) * 2 + low,
        "z": lax.rem(lax.div(shard, 2), 4),
    }
    return place, lax.rem(shard, 2)


def moved(place, axis, steps):
    steps = steps % 4
    if steps == 0:
        return place
    other = dict(place)
    other[axis] = lax.rem(place[axis] + steps, 4)
    return other


def device_at(place, core):
    high = lax.div(place["y"], 2)
    return (((place["x"] * 2 + high) * 4 + place["z"]) * 2 + core, lax.rem(place["y"], 2))


def greet(peers):
    barrier = pltpu.get_barrier_semaphore()
    for peer in peers:
        pl.semaphore_signal(barrier, inc=1, device_id=peer, device_id_type=MESH)
    pl.semaphore_wait(barrier, len(peers))


def part_columns(part, half, widths):
    start = 2 * sum(widths[:part]) + half * widths[part]
    return pl.ds(pl.multiple_of(start, LANES), widths[part])


def piece_of(ref, part, widths, place, core):
    return ref.at[
        place["x"],
        lax.div(place["y"], 2),
        place["z"],
        core,
        :,
        part_columns(part, lax.rem(place["y"], 2), widths),
    ]


def block_of(ref, part, widths, place, core, axis, half=None):
    where = {"x": place["x"], "y": lax.div(place["y"], 2), "z": place["z"]}
    if axis == "y":
        where["y"] = pl.ds(0, 2) if half is None else pl.ds(half, 1)
        columns = pl.ds(2 * sum(widths[:part]), 2 * widths[part])
    else:
        where[axis] = pl.ds(0, 4) if half is None else pl.ds(2 * half, 2)
        columns = part_columns(part, lax.rem(place["y"], 2), widths)
    return ref.at[where["x"], where["y"], where["z"], core, :, columns]


def remote(source, target, send, recv, device):
    return pltpu.make_async_remote_copy(
        src_ref=source,
        dst_ref=target,
        send_sem=send,
        recv_sem=recv,
        device_id=device,
        device_id_type=MESH,
    )


def cycle(value, steps):
    return lax.rem(value + steps, 4)


def turned_by(place, axis, steps):
    other = dict(place)
    other[axis] = cycle(place[axis], steps)
    return other


class Gatherer:
    SEMS = 3 + 3 + 8 + 8 + 16
    KINDS = {"one": 0, "two": 3, "three": 6, "four": 14, "twin": 22}

    def __init__(self, widths, place, core, own, full, send, recv, base):
        self.widths, self.place, self.core = widths, place, core
        self.own, self.full, self.send, self.recv, self.base = own, full, send, recv, base
        self.twin = device_at(place, 1 - core)

    def slot(self, part, kind, index):
        return self.base + part * self.SEMS + self.KINDS[kind] + index

    def push(self, source, target, slot, device):
        remote(source, target, self.send.at[slot], self.recv.at[slot], device).start()

    def arrived(self, region, slot):
        remote(region, region, self.send.at[slot], self.recv.at[slot], self.twin).wait_recv()

    def sent(self, region, slot):
        remote(region, region, self.send.at[slot], self.recv.at[slot], self.twin).wait_send()

    def block(self, part, place, half=None, core=None):
        core = self.core if core is None else core
        return block_of(self.full, part, self.widths, place, core, ORDERS[part][0], half)

    def keep(self, part):
        low = lax.rem(self.place["y"], 2)
        source = self.own.at[:, part_columns(part, low, self.widths)]
        target = piece_of(self.full, part, self.widths, self.place, self.core)
        return source, target, pltpu.make_async_copy(
            source, target, self.recv.at[self.base + 3 * self.SEMS + part]
        )

    def start(self):
        for part, (one, two, three) in enumerate(ORDERS):
            source, target, copy = self.keep(part)
            copy.start()
            for steps in (1, 3, 2):
                device = device_at(turned_by(self.place, one, steps), self.core)
                self.push(source, target, self.slot(part, "one", steps - 1), device)

    def second(self):
        for part, (one, two, three) in enumerate(ORDERS):
            self.keep(part)[2].wait()
            for steps in (1, 3, 2):
                origin = turned_by(self.place, one, 4 - steps)
                region = piece_of(self.full, part, self.widths, origin, self.core)
                self.arrived(region, self.slot(part, "one", steps - 1))
            block = self.block(part, self.place)
            for steps in (1, 3, 2):
                device = device_at(turned_by(self.place, two, steps), self.core)
                self.push(block, block, self.slot(part, "two", steps - 1), device)
        self.spread(0)

    def spread(self, steps):
        for part, (one, two, three) in enumerate(ORDERS):
            block = self.block(part, turned_by(self.place, two, 4 - steps))
            for index, way in enumerate((1, 3)):
                device = device_at(turned_by(self.place, three, way), self.core)
                self.push(block, block, self.slot(part, "three", index * 4 + steps), device)
            self.push(block, block, self.slot(part, "twin", steps), self.twin)

    def third(self, steps):
        for part, (one, two, three) in enumerate(ORDERS):
            block = self.block(part, turned_by(self.place, two, 4 - steps))
            self.arrived(block, self.slot(part, "two", steps - 1))
        self.spread(steps)

    def fourth(self, steps):
        for part, (one, two, three) in enumerate(ORDERS):
            side = turned_by(self.place, two, 4 - steps)
            for index, way in enumerate((1, 3)):
                origin = turned_by(side, three, 4 - way)
                block = self.block(part, origin)
                self.arrived(block, self.slot(part, "three", index * 4 + steps))
                half = self.block(part, origin, index)
                device = device_at(turned_by(self.place, three, way), self.core)
                self.push(half, half, self.slot(part, "four", index * 4 + steps), device)
                self.push(block, block, self.slot(part, "twin", way * 4 + steps), self.twin)

    def fifth(self, steps):
        for part, (one, two, three) in enumerate(ORDERS):
            origin = turned_by(turned_by(self.place, two, 4 - steps), three, 2)
            for index in range(2):
                half = self.block(part, origin, index)
                self.arrived(half, self.slot(part, "four", index * 4 + steps))
            block = self.block(part, origin)
            self.push(block, block, self.slot(part, "twin", 8 + steps), self.twin)

    def close(self):
        for part, (one, two, three) in enumerate(ORDERS):
            for way in range(4):
                for steps in range(4):
                    origin = moved(moved(self.place, two, -steps), three, -way)
                    region = self.block(part, origin, core=1 - self.core)
                    self.arrived(region, self.slot(part, "twin", way * 4 + steps))

    def drain(self):
        for part in range(3):
            piece = piece_of(self.full, part, self.widths, self.place, self.core)
            block = self.block(part, self.place)
            half = self.block(part, self.place, 0)
            for kind, region, count in (
                ("one", piece, 3),
                ("two", block, 3),
                ("three", block, 8),
                ("four", half, 8),
                ("twin", block, 16),
            ):
                for index in range(count):
                    self.sent(region, self.slot(part, kind, index))


class Reducer:
    SEMS = 8 + 8 + 3 + 3 + 1
    KINDS = {"mid": 0, "far": 8, "side": 16, "line": 19, "done": 22}

    def __init__(self, widths, place, core, buffers, out, send, recv, base=0):
        self.widths, self.place, self.core, self.base = widths, place, core, base
        self.acc, self.mid, self.far, self.side, self.line, self.done = [
            buffers[3 * i : 3 * i + 3] for i in range(6)
        ]
        self.out, self.send, self.recv = out, send, recv
        self.me = device_at(place, core)

    @staticmethod
    def scratch(widths):
        found = []
        for lead, half in (((4, 4), 1), ((2, 4), 2), ((2, 4), 1), ((3,), 1)):
            for width, (one, two, three) in zip(widths, ORDERS):
                if one == "y":
                    found.append(pltpu.VMEM(lead + (2 // half, 16, 2 * width), BF))
                else:
                    found.append(pltpu.VMEM(lead + (4 // half, 16, width), BF))
        found += [pltpu.VMEM((3, 16, width), BF) for width in widths]
        found += [pltpu.VMEM((16, width), BF) for width in widths]
        return found

    def slot(self, part, kind, index):
        return self.base + part * self.SEMS + self.KINDS[kind] + index

    def push(self, source, target, slot, device):
        remote(source, target, self.send.at[slot], self.recv.at[slot], device).start()

    def arrived(self, region, slot):
        remote(region, region, self.send.at[slot], self.recv.at[slot], self.me).wait_recv()

    def sent(self, region, slot):
        remote(region, region, self.send.at[slot], self.recv.at[slot], self.me).wait_send()

    def add(self, target, *terms):
        for index in range(target.shape[0]):
            total = target[index].astype(F32)
            for term in terms:
                total = total + term[index].astype(F32)
            target[index] = total.astype(BF)

    def half_of(self, ref, half):
        size = ref.shape[0] // 2
        return ref.at[pl.ds(half * size, size)]

    def far_out(self):
        for spot in range(4):
            for part, (one, two, three) in enumerate(ORDERS):
                for half, way in ((0, 3), (1, 1)):
                    self.push(
                        self.half_of(self.acc[part].at[2, spot], half),
                        self.mid[part].at[half, spot],
                        self.slot(part, "mid", half * 4 + spot),
                        device_at(moved(self.place, three, way), self.core),
                    )

    def pass_on(self, spot):
        for part, (one, two, three) in enumerate(ORDERS):
            for half, way in ((0, 3), (1, 1)):
                self.arrived(
                    self.mid[part].at[half, spot], self.slot(part, "mid", half * 4 + spot)
                )
                self.add(
                    self.half_of(self.acc[part].at[way, spot], half), self.mid[part].at[half, spot]
                )
                self.push(
                    self.acc[part].at[way, spot],
                    self.far[part].at[half, spot],
                    self.slot(part, "far", half * 4 + spot),
                    device_at(moved(self.place, three, way), self.core),
                )

    def gather_side(self, over, last):
        for part, (one, two, three) in enumerate(ORDERS):
            spot = cycle(self.place[two], over)
            for half in range(2):
                self.arrived(
                    self.far[part].at[half, spot], self.slot(part, "far", half * 4 + spot)
                )
            self.add(
                self.acc[part].at[0, spot], self.far[part].at[0, spot], self.far[part].at[1, spot]
            )

            def give(part=part, two=two, spot=spot):
                other = dict(self.place)
                other[two] = spot
                self.push(
                    self.acc[part].at[0, spot],
                    self.side[part].at[over - 1],
                    self.slot(part, "side", over - 1),
                    device_at(other, self.core),
                )

            if last is False:
                give()
            elif last is not True:
                pl.when(jnp.logical_not(last))(give)

    def piece(self, part, axis, spot):
        own = self.acc[part].at[0, self.place[ORDERS[part][1]]]
        if axis == "y":
            start = pl.multiple_of(lax.rem(spot["y"], 2) * self.widths[part], LANES)
            return own.at[lax.div(spot["y"], 2), :, pl.ds(start, self.widths[part])]
        return own.at[spot[axis]]

    def line_up(self):
        for part, (one, two, three) in enumerate(ORDERS):
            for over in range(3):
                self.arrived(self.side[part].at[over], self.slot(part, "side", over))
            own = self.acc[part].at[0, self.place[two]]
            self.add(own, self.side[part].at[0], self.side[part].at[1], self.side[part].at[2])
            for over in (2, 1, 3):
                spot = moved(self.place, one, over)
                self.push(
                    self.piece(part, one, spot),
                    self.line[part].at[over - 1],
                    self.slot(part, "line", over - 1),
                    device_at(spot, self.core),
                )

    def share(self):
        low = lax.rem(self.place["y"], 2)
        partner = (lax.axis_index("fsdp"), 1 - low)
        for part, (one, two, three) in enumerate(ORDERS):
            for over in range(3):
                self.arrived(self.line[part].at[over], self.slot(part, "line", over))
            total = self.piece(part, one, self.place)[...].astype(F32)
            for over in range(3):
                total = total + self.line[part][over].astype(F32)
            self.done[part][...] = total.astype(BF)
            columns = part_columns(part, low, self.widths)
            self.push(
                self.done[part], self.out.at[:, columns], self.slot(part, "done", 0), partner
            )
            self.out[:, columns] = self.done[part][...]

    def close(self):
        low = lax.rem(self.place["y"], 2)
        for part, (one, two, three) in enumerate(ORDERS):
            self.arrived(
                self.out.at[:, part_columns(part, 1 - low, self.widths)],
                self.slot(part, "done", 0),
            )
            for half in range(2):
                for spot in range(4):
                    index = half * 4 + spot
                    self.sent(self.mid[part].at[half, spot], self.slot(part, "mid", index))
                    self.sent(self.far[part].at[half, spot], self.slot(part, "far", index))
            for over in range(3):
                self.sent(self.side[part].at[over], self.slot(part, "side", over))
                self.sent(self.line[part].at[over], self.slot(part, "line", over))
            self.sent(self.done[part], self.slot(part, "done", 0))


class Maker:
    def __init__(self, reducer, sources, extra, chunk):
        self.red, self.sources, self.extra, self.chunk = reducer, sources, extra, chunk
        self.main = sum(item[1].shape[1] for item in sources)

    def pack_tail(self):
        start = 0
        pieces = []
        for turned, right in self.sources:
            pieces.append((start, start + right.shape[1], turned, right))
            start += right.shape[1]
        for index in range(8):
            low, high = index * self.chunk, (index + 1) * self.chunk
            for first, last, turned, right in pieces:
                a, b = max(low, first), min(high, last)
                if a < b:
                    value = dot(turned[1][...], right[:, a - first : b - first])
                    self.scatter(index, a - low, value)
            if high > self.main:
                a = max(low, self.main)
                self.scatter(index, a - low, jnp.zeros((TAIL, high - a), F32))

    def scatter(self, index, start, value):
        for tile in range(value.shape[1] // LANES):
            self.extra[start // LANES + tile, pl.ds(index, TAIL, stride=8), :] = value[
                :, tile * LANES : (tile + 1) * LANES
            ]

    def rows(self, ref, part, ahead):
        place, core = self.red.place, self.red.core
        three = ORDERS[part][2]
        spot = cycle(place[three], ahead)
        if len(ref.shape) == 2:
            if three == "z":
                groups = [outer * 8 + spot * 2 + core for outer in range(8)]
            elif three == "x":
                groups = [spot * 16 + inner * 2 + core for inner in range(8)]
            else:
                high = lax.div(spot, 2) * 8
                groups = [x * 16 + high + z * 2 + core for x in range(4) for z in range(4)]
            found = [ref[pl.ds(pl.multiple_of(group * 16, 16), 16)] for group in groups]
            return jnp.concatenate(found, axis=0)
        if three == "z":
            value = ref[:, :, spot, core]
        elif three == "x":
            value = ref[spot, :, :, core]
        else:
            value = ref[:, lax.div(spot, 2), :, core]
        return value.reshape(-1, ref.shape[-1])

    def columns(self, part, half, ahead):
        width = self.red.widths[part]
        low = 2 * sum(self.red.widths[:part]) + half * width
        high = low + width
        first = 0
        found = []
        for turned, right in self.sources:
            last = first + right.shape[1]
            a, b = max(low, first), min(high, last)
            if a < b:
                left = self.rows(turned[0], part, ahead)
                found.append(dot(left, right[:, a - first : b - first]).astype(BF))
            first = last
        a, b = max(low, first), min(high, first + self.chunk)
        if a < b:
            for tile in range((a - first) // LANES, (b - first) // LANES):
                found.append(self.rows(self.extra.at[tile], part, ahead).astype(BF))
        a = max(low, first + self.chunk)
        if a < high:
            found.append(jnp.zeros((found[0].shape[0], high - a), BF))
        return found[0] if len(found) == 1 else jnp.concatenate(found, axis=1)

    def make(self, part, ahead):
        red, width = self.red, self.red.widths[part]
        acc = red.acc[part]
        three = ORDERS[part][2]
        if three == "z":
            for half in range(2):
                value = self.columns(part, half, ahead).reshape(4, 2, 16, width)
                for high in range(2):
                    acc[ahead, 2 * high + half] = value[:, high]
        elif three == "x":
            for half in range(2):
                value = self.columns(part, half, ahead).reshape(2, 4, 16, width)
                for spot in range(4):
                    acc[ahead, spot, :, :, half * width : (half + 1) * width] = value[:, spot]
        else:
            low = lax.rem(cycle(red.place["y"], ahead), 2)
            for half in range(2):

                @pl.when(low == half)
                def _(half=half):
                    value = self.columns(part, half, ahead).reshape(4, 4, 16, width)
                    for spot in range(4):
                        acc[ahead, spot] = value[spot]


SWAP_ORDER = (9, 11, 5, 13, 7, 15, 1, 3, 8, 10, 4, 12, 6, 14, 2)


class Swapper:
    def __init__(self, place, core, own, full, send, recv, base):
        self.place, self.core = place, core
        self.own, self.full, self.send, self.recv, self.base = own, full, send, recv, base
        self.low = lax.rem(place["y"], 2)
        self.mine = (place["z"] * 2 + core) * 2 + self.low
        self.group = lax.div(lax.axis_index("fsdp"), 8) * 8

    def member(self, k, sign=1):
        z = lax.rem(self.place["z"] + (4 + sign * (k // 4)), 4)
        core = lax.rem(self.core + (k // 2) % 2, 2)
        low = lax.rem(self.low + k % 2, 2)
        return (z * 2 + core) * 2 + low

    def device(self, index):
        return (self.group + lax.div(index, 2), lax.rem(index, 2))

    def peers(self):
        return [self.device(self.member(k)) for k in range(1, 16)]

    def view(self, ref, index, micro):
        if micro is None:
            return ref.at[index]
        return ref.at[index, pl.ds(micro * 128, 128)]

    def start(self, micro=None):
        for k in SWAP_ORDER:
            target = self.member(k)
            remote(
                self.view(self.own, target, micro),
                self.view(self.full, self.mine, micro),
                self.send.at[self.base + k],
                self.recv.at[self.base + k],
                self.device(target),
            ).start()
        pltpu.make_async_copy(
            self.view(self.own, self.mine, micro),
            self.view(self.full, self.mine, micro),
            self.send.at[self.base],
        ).start()

    def finish(self, micro=None):
        pltpu.make_async_copy(
            self.view(self.own, self.mine, micro),
            self.view(self.full, self.mine, micro),
            self.send.at[self.base],
        ).wait()
        for k in range(1, 16):
            region = self.view(self.full, self.member(k, -1), micro)
            remote(
                region,
                region,
                self.send.at[self.base + k],
                self.recv.at[self.base + k],
                self.device(self.mine),
            ).wait_recv()

    def drain(self, micro=None):
        for k in range(1, 16):
            region = self.view(self.own, self.member(k), micro)
            remote(
                region,
                region,
                self.send.at[self.base + k],
                self.recv.at[self.base + k],
                self.device(self.mine),
            ).wait_send()


def line_peers(place, core):
    peers = []
    for axis in AXES:
        for steps in (1, 2, 3):
            peers.append(device_at(moved(place, axis, steps), core))
    return peers


D = 1152
HEADS = 16
HEAD_DIM = 72
FF = 4304
ROW = 2048
EPS = 1e-06
NEG = -1e30
SCALE = HEAD_DIM**-0.5
LEAD = 1024
TAIL = 128
PACK = 3 * HEAD_DIM
WIDE = 256
VALUE_LANE = 16
FF_PAD = 4352
QKV = HEADS * PACK
ATTN_MAIN = QKV + D
ATTN_CHUNK = 640
ATTN_TOTAL = 5376
MLP_MAIN = 2 * FF_PAD
MLP_CHUNK = 1152
MLP_TOTAL = 9984
ATTN_WIDTHS = (896, 896, 896)
MLP_WIDTHS = (1664, 1664, 1664)
FIRST = 2304
FIRST_CHUNK = 640
FIRST_TOTAL = 5376
FIRST_WIDTHS = (896, 896, 896)
FIRST_STEP = 768
SECOND = FF_PAD - FIRST
SECOND_CHUNK = 512
SECOND_TOTAL = 4608
SECOND_WIDTHS = (768, 768, 768)
SECOND_STEP = 512
LOG2E = 1.4426950408889634
QUERIES = 512
KEYS = 512
BLOCKS = ROW // QUERIES
TANH_A = 0.7978845608028654
TANH_B = 0.044715


def dot(left, right):
    return jnp.dot(left, right, preferred_element_type=F32)


def dot_nt(left, right):
    return lax.dot_general(left, right, (((1,), (1,)), ((), ())), preferred_element_type=F32)


def dot_tn(left, right):
    return lax.dot_general(left, right, (((0,), (0,)), ((), ())), preferred_element_type=F32)


def origin(index):
    lead = (index >> 4) * 18 + (index & 15)
    rest = index - LEAD
    tail = (rest >> 1) * 18 + 16 + (rest & 1)
    return jnp.where(index < LEAD, lead, tail)


def iota(shape, axis):
    return lax.broadcasted_iota(jnp.int32, shape, axis)


def onehot(mask):
    return mask.astype(F32).astype(BF)


def normal(values):
    center = values - jnp.mean(values, axis=-1, keepdims=True)
    rate = lax.rsqrt(jnp.mean(center * center, axis=-1, keepdims=True) + EPS)
    return center * rate, rate


def normal_back(unit, rate, gain, grad):
    inner = grad * gain
    first = jnp.mean(inner, axis=-1, keepdims=True)
    second = jnp.mean(inner * unit, axis=-1, keepdims=True)
    return rate * (inner - first - unit * second)


def column_total(values):
    return jnp.sum(values, axis=0, keepdims=True)


def lanes(start, size):
    return pl.ds(pl.multiple_of(start, LANES), size)


def params(limit=60):
    return pltpu.CompilerParams(vmem_limit_bytes=limit << 20)


def head_place(head):
    spot = iota((LANES, D), 0) - VALUE_LANE
    inside = (spot >= 0) & (spot < HEAD_DIM)
    return onehot(inside & (origin(iota((LANES, D), 1)) == HEAD_DIM * head + spot))


def head_pick(head):
    spot = iota((D, LANES), 1) - VALUE_LANE
    inside = (spot >= 0) & (spot < HEAD_DIM)
    return onehot(inside & (origin(iota((D, LANES), 0)) == HEAD_DIM * head + spot))


def unmix(value):
    return onehot(origin(iota((D, LANES), 0)) == value * LANES + iota((D, LANES), 1))


def mesh_params(tag, limit=62):
    return pltpu.CompilerParams(
        collective_id=tag, has_side_effects=True, vmem_limit_bytes=limit << 20
    )


class Twin:
    def __init__(self, place, core, send, recv, base):
        self.core, self.device = core, device_at(place, 1 - core)
        self.send, self.recv, self.base = send, recv, base
        self.items = []

    def half(self, ref, axis, core):
        size = ref.shape[axis] // 2
        if axis == 0:
            return ref.at[pl.ds(pl.multiple_of(core * size, size), size)]
        lead = (slice(None),) * (len(ref.shape) - 1)
        return ref.at[lead + (pl.ds(pl.multiple_of(core * size, LANES), size),)]

    def give(self, source, target, axis):
        index = self.base + 2 * len(self.items)
        place = self.half(target, axis, self.core)
        pltpu.make_async_copy(source, place, self.recv.at[index + 1]).start()
        remote(source, place, self.send.at[index], self.recv.at[index], self.device).start()
        self.items.append((source, target, axis, index))

    def ready(self):
        for source, target, axis, index in self.items:
            place = self.half(target, axis, self.core)
            pltpu.make_async_copy(source, place, self.recv.at[index + 1]).wait()
            other = self.half(target, axis, 1 - self.core)
            remote(
                other, other, self.send.at[index], self.recv.at[index], self.device
            ).wait_recv()

    def drain(self):
        for source, target, axis, index in self.items:
            place = self.half(target, axis, self.core)
            remote(
                place, place, self.send.at[index], self.recv.at[index], self.device
            ).wait_send()


def back_kernel(
    go,
    dpre,
    active,
    h_main,
    h_tail,
    g_main,
    g_tail,
    picture,
    packed_ref,
    keep_ref,
    share_ref,
    dheads,
    go_all,
    grads,
    dpre_all,
    active_all,
    h_main_all,
    h_tail_all,
    g_main_all,
    g_tail_all,
    extra,
    keys,
    queries,
    ids,
    dkeys,
    dvalues,
    found,
    row_ref,
    *rest,
):
    buffers, (send, recv, local) = rest[:-3], rest[-3:]
    place, core = here()
    red = Reducer(FIRST_WIDTHS, place, core, buffers, share_ref, send, recv)
    base = 3 * Reducer.SEMS
    swap_in = Swapper(place, core, go, go_all, send, recv, base)
    outs = [Swapper(place, core, grads, dheads, send, recv, base + 16 + 16 * m) for m in range(2)]
    twin = Twin(place, core, send, recv, base + 48)
    greet(line_peers(place, core) + swap_only(swap_in))
    swap_in.start()
    for source, target, axis in (
        (h_main, h_main_all, 5),
        (h_tail, h_tail_all, 1),
        (g_main, g_main_all, 5),
        (g_tail, g_tail_all, 1),
        (dpre.at[:, pl.ds(0, FIRST)], dpre_all, 0),
        (active.at[:, pl.ds(0, FIRST)], active_all, 0),
    ):
        twin.give(source, target, axis)
    maker = Maker(
        red,
        [((h_main_all, h_tail_all), dpre_all), ((g_main_all, g_tail_all), active_all)],
        extra,
        FIRST_CHUNK,
    )
    ids_in = fetch_ids(picture, found, local.at[0])
    ids_in.start()
    ids_in.wait()
    for micro in range(2):
        row_ref[micro] = found[micro : micro + 1].astype(F32)
    twin.ready()
    maker.pack_tail()
    for part in range(3):
        maker.make(part, 2)
    red.far_out()

    def others(index, carry):
        ahead = cycle(index, 3)
        for part in range(3):
            maker.make(part, ahead)
        return carry

    lax.fori_loop(0, 3, others, 0)
    swap_in.finish()

    def block(step, carry):
        row = lax.div(step, BLOCKS)
        index = lax.rem(step, BLOCKS)
        tokens = pl.ds(pl.multiple_of(row * 128, 128), 128)

        @pl.when(index == 0)
        def _():
            packed = packed_ref[:, tokens, :].reshape(ROW, WIDE)
            split_packed(packed, keys, queries)
            for part in range(ROW // LANES):
                span = slice(part * LANES, (part + 1) * LANES)
                ids[span, :] = column_ids(row_ref[row, :, span])
            dkeys[...] = jnp.zeros_like(dkeys)
            dvalues[...] = jnp.zeros_like(dvalues)

        rows = pl.ds(pl.multiple_of(index * QUERIES, QUERIES), QUERIES)
        groups = pl.ds(index * (QUERIES // 128), QUERIES // 128)
        query = queries[rows, :]
        back = go_all[groups, tokens, :].reshape(QUERIES, LANES)
        mine = row_ref[row, :, lanes(index * QUERIES, QUERIES)]
        kept = keep_ref[row, rows, :]
        inner = jnp.sum(back.astype(F32) * kept, axis=1, keepdims=True)
        lane = iota((QUERIES, LANES), 1)
        stats = jnp.transpose(jnp.where(lane == 0, kept, inner))
        logsum = stats[0:1]
        inner = stats[1:2]
        total = jnp.zeros((QUERIES, LANES), F32)
        for part in range(ROW // KEYS):
            span = slice(part * KEYS, (part + 1) * KEYS)
            blocks = slice(part * KEYS // 128, (part + 1) * KEYS // 128)
            value = packed_ref[blocks, tokens, LANES:].reshape(KEYS, LANES)
            allowed = jnp.concatenate([ids[span, :]] * (QUERIES // LANES), axis=1)
            score = dot_nt(keys[span, :], query) * (SCALE * LOG2E) - logsum
            prob = jnp.exp2(jnp.where(allowed == mine, score, NEG))
            grad = (prob * (dot_nt(value, back) - inner)).astype(BF)
            dvalues[span, :] += dot(prob.astype(BF), back)
            dkeys[span, :] += dot(grad, query)
            total = total + dot_tn(grad, keys[span, :])
        total = total * SCALE
        moved_q = jnp.concatenate(
            [
                jnp.zeros((QUERIES, HEAD_DIM), F32),
                total[:, :HEAD_DIM],
                jnp.zeros((QUERIES, WIDE - 2 * HEAD_DIM), F32),
            ],
            axis=1,
        )
        grads[groups, tokens, :] = moved_q.astype(BF).reshape(QUERIES // 128, 128, WIDE)

        @pl.when(index == BLOCKS - 1)
        def _():
            wide = jnp.concatenate([dkeys[...] * SCALE, dvalues[...]], axis=1)
            lane = iota((ROW, WIDE), 1)
            old = grads[:, tokens, :].reshape(ROW, WIDE)
            inside = (lane >= HEAD_DIM) & (lane < 2 * HEAD_DIM)
            grads[:, tokens, :] = jnp.where(inside, old, wide.astype(BF)).reshape(16, 128, WIDE)
            for micro in range(2):
                pl.when(row == micro)(functools.partial(outs[micro].start, micro))

        @pl.when(step < 4)
        def _():
            red.pass_on(step)

        @pl.when(step >= 4)
        def _():
            red.gather_side(lax.rem(step - 4 + 1, 4), step == 7)

        return carry

    lax.fori_loop(0, 2 * BLOCKS, block, 0)
    red.line_up()
    red.share()
    red.close()
    for micro in range(2):
        outs[micro].finish(micro)
    swap_in.drain()
    for micro in range(2):
        outs[micro].drain(micro)
    twin.drain()


def attend_back_reduce(go, dpre, active, turned, packed, keep, picture, tag):
    any_ = pl.BlockSpec(memory_space=pl.ANY)
    vmem = pl.BlockSpec(memory_space=pltpu.VMEM)
    sems = 3 * Reducer.SEMS + 48 + 12
    return pl.pallas_call(
        back_kernel,
        out_shape=(
            jax.ShapeDtypeStruct((16, FIRST_TOTAL), BF),
            jax.ShapeDtypeStruct((16, 256, WIDE), BF),
        ),
        in_specs=[any_] * 8 + [vmem] * 2,
        out_specs=(vmem, any_),
        scratch_shapes=[
            pltpu.VMEM((16, 256, LANES), BF),
            pltpu.VMEM((16, 256, WIDE), BF),
            pltpu.VMEM((512, FIRST), BF),
            pltpu.VMEM((512, FIRST), BF),
            pltpu.VMEM((4, 2, 4, 2, 16, 512), BF),
            pltpu.VMEM((TAIL, 512), BF),
            pltpu.VMEM((4, 2, 4, 2, 16, 512), BF),
            pltpu.VMEM((TAIL, 512), BF),
            pltpu.VMEM((FIRST_CHUNK // LANES, LEAD, LANES), F32),
            pltpu.VMEM((ROW, LANES), BF),
            pltpu.VMEM((ROW, LANES), BF),
            pltpu.VMEM((ROW, LANES), F32),
            pltpu.VMEM((ROW, LANES), F32),
            pltpu.VMEM((ROW, LANES), F32),
            pltpu.VMEM((2, ROW), jnp.int32),
            pltpu.VMEM((2, 1, ROW), F32),
        ]
        + Reducer.scratch(FIRST_WIDTHS)
        + [
            pltpu.SemaphoreType.DMA((sems,)),
            pltpu.SemaphoreType.DMA((sems,)),
            pltpu.SemaphoreType.DMA((1,)),
        ],
        compiler_params=mesh_params(tag),
        name="attend_back_reduce",
    )(go, dpre, active, *turned, picture, packed, keep)


VEC_ROWS = 16
VEC_QKV = 6
VEC_UP = 9


def spread_tail(source, chunk, wide, tail):
    for tile in range(chunk // LANES):
        wide[tile] = source(tile).astype(F32)
        for index in range(8):
            start = index * chunk + tile * LANES
            picked = wide[tile, pl.ds(index, TAIL, stride=8), :]
            tail[:, start : start + LANES] = picked.astype(BF)


def open_kernel(
    slab,
    tokens_ref,
    cotangent_ref,
    *refs,
):
    lines, rest = refs[:8], refs[8:]
    run_open(slab, tokens_ref, cotangent_ref, lines, *rest)


def run_open(
    slab,
    tokens_ref,
    cotangent_ref,
    lines,
    heads_ref,
    x_ref,
    g_ref,
    h_main_ref,
    h_tail_ref,
    tail_ref,
    out_tail_ref,
    mixed_vec_ref,
    weight_out,
    full,
    low,
    flat,
    wide,
    tail,
    vec_ref,
    send,
    recv,
    local,
):
    place, core = here()
    red = Gatherer(ATTN_WIDTHS, place, core, slab, full, send, recv, 0)
    greet(line_peers(place, core) + [device_at(place, 1 - core)])
    red.start()
    for index, line in enumerate(lines):
        vec_ref[index : index + 1, :] = line[...].reshape(1, D)

    def mix(index, carry):
        columns = lanes(index * LANES, LANES)
        column = onehot(iota((D, LANES), 0) == origin(index * LANES + iota((D, LANES), 1)))
        x_ref[:, columns] = dot(tokens_ref[...], column).astype(BF)
        g_ref[:, columns] = dot(cotangent_ref[...], column).astype(BF)
        mixed_vec_ref[:, columns] = jnp.dot(
            vec_ref[...],
            column.astype(F32),
            precision=lax.Precision.HIGHEST,
            preferred_element_type=F32,
        )
        return carry

    lax.fori_loop(0, 9, mix, 0)
    red.second()
    unit, _ = normal(x_ref[...].astype(F32))
    low[...] = (unit * mixed_vec_ref[0:1] + mixed_vec_ref[1:2]).astype(BF)
    for steps in (1, 2, 3):
        red.third(steps)
    turned = jnp.transpose(low[...])
    h_main_ref[...] = turned[:LEAD].reshape(4, 2, 4, 2, 16, 256)
    h_tail_ref[...] = turned[LEAD:]
    for steps in range(4):
        red.fourth(steps)
    for steps in range(4):
        red.fifth(steps)
    red.close()
    leave = pltpu.make_async_copy(full, weight_out, local.at[0])
    leave.start()

    def packed(tile):
        start = ATTN_MAIN + tile * LANES
        return full[:, :, :, :, :, start : start + LANES].reshape(LEAD, LANES)

    spread_tail(packed, ATTN_CHUNK, wide, tail)
    tail_ref[...] = tail[:, :QKV]
    out_tail_ref[...] = tail[:, QKV:ATTN_MAIN]

    def columns(index, carry):
        span = lanes(index * 384, 384)
        weight = full[:, :, :, :, :, span].reshape(LEAD, 384)
        flat[:, span] = dot(low[:, :LEAD], weight) + dot(low[:, LEAD:], tail[:, span])
        return carry

    lax.fori_loop(0, QKV // 384, columns, 0)
    for head in range(HEADS):
        span = slice(head * HEAD_DIM, (head + 1) * HEAD_DIM)
        bias = jnp.concatenate(
            [jnp.zeros((1, HEAD_DIM), F32), vec_ref[6:7, span], vec_ref[7:8, span]], axis=1
        )
        block = flat[:, PACK * head : PACK * head + PACK] + bias
        heads_ref[head] = jnp.concatenate(
            [block, jnp.zeros((256, WIDE - PACK), F32)], axis=1
        ).astype(BF)
    red.drain()
    leave.wait()


def open_layer(slab, tokens, cotangent, lines, tag):
    any_ = pl.BlockSpec(memory_space=pl.ANY)
    vmem = pl.BlockSpec(memory_space=pltpu.VMEM)
    sems = 3 * Gatherer.SEMS + 3
    full = (4, 2, 4, 2, 16, ATTN_TOTAL)
    return pl.pallas_call(
        open_kernel,
        out_shape=(
            jax.ShapeDtypeStruct((HEADS, 256, WIDE), BF),
            jax.ShapeDtypeStruct((256, D), BF),
            jax.ShapeDtypeStruct((256, D), BF),
            jax.ShapeDtypeStruct((4, 2, 4, 2, 16, 256), BF),
            jax.ShapeDtypeStruct((TAIL, 256), BF),
            jax.ShapeDtypeStruct((TAIL, QKV), BF),
            jax.ShapeDtypeStruct((TAIL, D), BF),
            jax.ShapeDtypeStruct((8, D), F32),
            jax.ShapeDtypeStruct(full, BF),
        ),
        in_specs=[any_] + [vmem] * 10,
        out_specs=(vmem,) * 8 + (any_,),
        scratch_shapes=[
            pltpu.VMEM(full, BF),
            pltpu.VMEM((256, D), BF),
            pltpu.VMEM((256, QKV), F32),
            pltpu.VMEM((ATTN_CHUNK // LANES, LEAD, LANES), F32),
            pltpu.VMEM((TAIL, 8 * ATTN_CHUNK), BF),
            pltpu.VMEM((8, D), F32),
            pltpu.SemaphoreType.DMA((sems,)),
            pltpu.SemaphoreType.DMA((sems,)),
            pltpu.SemaphoreType.DMA((1,)),
        ],
        compiler_params=mesh_params(tag),
        name="open_layer",
    )(slab, tokens, cotangent, *lines)


def column_ids(row_ids):
    size = row_ids.shape[1]
    return jnp.transpose(jnp.broadcast_to(row_ids, (LANES, size)))


def fetch_ids(picture, found, sem):
    start = pl.multiple_of(lax.div(lax.axis_index("fsdp"), 8) * ROW, ROW)
    return pltpu.make_async_copy(picture.at[:, pl.ds(start, ROW)], found, sem)


def split_packed(packed, keys, queries):
    lane = iota((ROW, LANES), 1)
    zero = jnp.zeros((ROW, LANES), BF)
    keys[...] = jnp.where(lane < HEAD_DIM, packed[:, :LANES], zero)
    queries[...] = jnp.concatenate(
        [packed[:, HEAD_DIM : 2 * HEAD_DIM], jnp.zeros((ROW, LANES - HEAD_DIM), BF)], axis=1
    )


def swap_only(swapper):
    return [swapper.device(swapper.member(k)) for k in range(1, 16) if k not in (1, 4, 8, 12)]


def attend_kernel(
    heads,
    slab,
    picture,
    packed_ref,
    keep_ref,
    o_all,
    full,
    o_own,
    keys,
    queries,
    values,
    scores,
    found,
    row_ref,
    send,
    recv,
    local,
):
    place, core = here()
    red = Gatherer(FIRST_WIDTHS, place, core, slab, full, send, recv, 0)
    base = 3 * Gatherer.SEMS + 3
    swap_in = Swapper(place, core, heads, packed_ref, send, recv, base)
    outs = [Swapper(place, core, o_own, o_all, send, recv, base + 16 + 16 * m) for m in range(2)]
    greet(line_peers(place, core) + swap_only(swap_in))
    red.start()
    swap_in.start()
    ids_in = fetch_ids(picture, found, local.at[0])
    ids_in.start()
    ids_in.wait()
    for micro in range(2):
        row_ref[micro] = found[micro : micro + 1].astype(F32)
    red.second()
    for steps in (1, 2, 3):
        red.third(steps)
    swap_in.finish()

    def block(step, carry):
        row = lax.div(step, 8)
        index = lax.rem(step, 8)
        tokens = pl.ds(pl.multiple_of(row * 128, 128), 128)

        @pl.when(index == 0)
        def _():
            packed = packed_ref[:, tokens, :].reshape(ROW, WIDE)
            split_packed(packed, keys, queries)
            lane = iota((ROW, LANES), 1)
            values[...] = jnp.where(
                lane == LANES - 1, jnp.ones((ROW, LANES), BF), packed[:, LANES:]
            )

        rows = pl.ds(pl.multiple_of(index * 256, 256), 256)
        query = queries[rows, :]
        mine = column_ids(row_ref[row, :, lanes(index * 256, 256)])
        mine = jnp.concatenate([mine] * (KEYS // LANES), axis=1)
        top = jnp.full((256, LANES), NEG, F32)
        for part in range(ROW // KEYS):
            span = slice(part * KEYS, (part + 1) * KEYS)
            score = dot_nt(query, keys[span, :])
            score = jnp.where(mine == row_ref[row, :, span], score, NEG)
            scores[:, span] = score
            for lane_block in range(KEYS // LANES):
                top = jnp.maximum(top, score[:, lane_block * LANES : (lane_block + 1) * LANES])
        top = jnp.max(top, axis=1, keepdims=True)
        total = jnp.zeros((256, LANES), F32)
        for part in range(ROW // KEYS):
            span = slice(part * KEYS, (part + 1) * KEYS)
            expo = jnp.exp2((scores[:, span] - top) * (SCALE * LOG2E))
            total = total + dot(expo.astype(BF), values[span, :])
        mass = total[:, LANES - 1 :]
        total = total / mass
        o_own[pl.ds(index * 2, 2), tokens, :] = total.astype(BF).reshape(2, 128, LANES)
        lane = iota((256, LANES), 1)
        logsum = top * (SCALE * LOG2E) + jnp.log2(mass)
        keep_ref[row, rows, :] = jnp.where(lane == 0, logsum, total)

        @pl.when(lax.rem(step, 4) == 0)
        def _():
            red.fourth(lax.div(step, 4))

        for micro in range(2):
            pl.when(step == 8 * micro + 7)(functools.partial(outs[micro].start, micro))
        return carry

    lax.fori_loop(0, 16, block, 0)
    for steps in range(4):
        red.fifth(steps)
    red.close()
    for micro in range(2):
        outs[micro].finish(micro)
    red.drain()
    swap_in.drain()
    for micro in range(2):
        outs[micro].drain(micro)


def attend_gather(heads, slab, picture, tag):
    any_ = pl.BlockSpec(memory_space=pl.ANY)
    vmem = pl.BlockSpec(memory_space=pltpu.VMEM)
    sems = 3 * Gatherer.SEMS + 3 + 48
    return pl.pallas_call(
        attend_kernel,
        out_shape=(
            jax.ShapeDtypeStruct((16, 256, WIDE), BF),
            jax.ShapeDtypeStruct((2, ROW, LANES), F32),
            jax.ShapeDtypeStruct((16, 256, LANES), BF),
            jax.ShapeDtypeStruct((4, 2, 4, 2, 16, FIRST_TOTAL), BF),
        ),
        in_specs=[any_] * 3,
        out_specs=(vmem, vmem, any_, any_),
        scratch_shapes=[pltpu.VMEM((16, 256, LANES), BF)]
        + [pltpu.VMEM((ROW, LANES), BF)] * 3
        + [
            pltpu.VMEM((256, ROW), F32),
            pltpu.VMEM((2, ROW), jnp.int32),
            pltpu.VMEM((2, 1, ROW), F32),
            pltpu.SemaphoreType.DMA((sems,)),
            pltpu.SemaphoreType.DMA((sems,)),
            pltpu.SemaphoreType.DMA((1,)),
        ],
        compiler_params=mesh_params(tag),
        name="attend_gather",
    )(heads, slab, picture)


def middle_kernel(
    attn,
    first,
    slab,
    o_ref,
    x_ref,
    g_ref,
    out_b_ref,
    vec_ref,
    bias_ref,
    mixed_ref,
    do_ref,
    dmid_ref,
    dy_ref,
    gvec_ref,
    gbias_ref,
    dpre_ref,
    active_ref,
    h_main_ref,
    h_tail_ref,
    g_main_ref,
    g_tail_ref,
    o_main_ref,
    o_tail_ref,
    out_a,
    weights,
    full,
    o_perm,
    mid,
    h2,
    result,
    dh2,
    wide,
    tail,
    bias,
    send,
    recv,
    local,
):
    place, core = here()
    red = Gatherer(SECOND_WIDTHS, place, core, slab, full, send, recv, 0)
    out_in = pltpu.make_async_copy(attn.at[:, pl.ds(QKV, D)], out_a, local.at[0])
    out_in.start()
    first_in = pltpu.make_async_copy(first, weights, local.at[1])
    first_in.start()
    greet(line_peers(place, core) + [device_at(place, 1 - core)])
    red.start()
    bias[...] = jnp.zeros_like(bias)
    bias[:, :FF] = bias_ref[...].reshape(1, FF)
    mid[...] = jnp.zeros_like(mid)

    def gather_head(head, carry):
        mid[...] += dot(o_ref[head], head_place(head))
        return carry

    lax.fori_loop(0, HEADS, gather_head, 0)
    o_perm[...] = mid[...].astype(BF)
    red.second()
    out_in.wait()
    for part in range(3):
        columns = slice(384 * part, 384 * part + 384)
        value = dot(o_perm[:, :LEAD], out_a[:, columns])
        value = value + dot(o_perm[:, LEAD:], out_b_ref[:, columns])
        mid[:, columns] = x_ref[:, columns].astype(F32) + value + vec_ref[4:5, columns]
    unit, _ = normal(mid[...])
    h2[...] = (unit * vec_ref[2:3] + vec_ref[3:4]).astype(BF)
    for steps in (1, 2, 3):
        red.third(steps)

    def turn(value, main, rest):
        turned = jnp.transpose(value)
        main[...] = turned[:LEAD].reshape(4, 2, 4, 2, 16, 256)
        rest[...] = turned[LEAD:]

    turn(o_perm[...], o_main_ref, o_tail_ref)
    turn(h2[...], h_main_ref, h_tail_ref)
    turn(g_ref[...], g_main_ref, g_tail_ref)
    result[...] = jnp.zeros_like(result)
    dh2[...] = jnp.zeros_like(dh2)
    first_in.wait()

    def tile_of(ref, main):
        def read(tile):
            start = main + tile * LANES
            return ref[:, :, :, :, :, start : start + LANES].reshape(LEAD, LANES)

        return read

    spread_tail(tile_of(weights, 2 * FIRST), FIRST_CHUNK, wide, tail)
    red.fourth(0)
    red.fourth(1)

    def chunk(ref, span, width, index, size):
        up_place = lanes(index * size, size)
        down_place = lanes(width + index * size, size)
        place_all = lanes(span + index * size, size)
        up = ref[:, :, :, :, :, up_place].reshape(LEAD, size)
        down = ref[:, :, :, :, :, down_place].reshape(LEAD, size)
        up_tail = tail[:, up_place]
        down_tail = tail[:, down_place]
        pre = dot(h2[:, :LEAD], up) + dot(h2[:, LEAD:], up_tail) + bias[:, place_all]
        square = pre * pre
        bend = jnp.tanh(TANH_A * pre * (1.0 + TANH_B * square))
        half = 0.5 * (1.0 + bend)
        active = (pre * half).astype(BF)
        slope = half + 0.5 * pre * (1.0 - bend * bend) * (TANH_A * (1.0 + 3.0 * TANH_B * square))
        back = dot(g_ref[:, :LEAD], down) + dot(g_ref[:, LEAD:], down_tail)
        dpre = (back * slope).astype(BF)
        active_ref[:, place_all] = active
        dpre_ref[:, place_all] = dpre
        active_t = jnp.transpose(active)
        dpre_t = jnp.transpose(dpre)
        result[:LEAD] += dot(down, active_t)
        result[LEAD:] += dot(down_tail, active_t)
        dh2[:LEAD] += dot(up, dpre_t)
        dh2[LEAD:] += dot(up_tail, dpre_t)
        gbias_ref[:, place_all] = column_total(dpre.astype(F32))

    def early(index, carry):
        chunk(weights, 0, FIRST, index, FIRST_STEP)

        @pl.when(index == 0)
        def _():
            red.fourth(2)
            red.fourth(3)

        @pl.when(index == 1)
        def _():
            for steps in range(4):
                red.fifth(steps)

        return carry

    lax.fori_loop(0, FIRST // FIRST_STEP, early, 0)
    red.close()
    spread_tail(tile_of(full, 2 * SECOND), SECOND_CHUNK, wide, tail)

    def late(index, carry):
        chunk(full, FIRST, SECOND, index, SECOND_STEP)
        return carry

    lax.fori_loop(0, SECOND // SECOND_STEP, late, 0)
    red.drain()
    gain = vec_ref[2:3]
    unit, rate = normal(mid[...])
    grad = jnp.transpose(dh2[...])
    gvec_ref[...] = jnp.zeros_like(gvec_ref)
    gvec_ref[0:1] = column_total(grad * unit)
    gvec_ref[1:2] = column_total(grad)
    gvec_ref[3:4] = column_total(g_ref[...].astype(F32))
    dmid = g_ref[...].astype(F32) + normal_back(unit, rate, gain, grad)
    dmid_ref[...] = dmid
    dlow = dmid.astype(BF)
    dy_ref[...] = dlow
    gvec_ref[2:3] = column_total(dlow.astype(F32))
    mixed_ref[...] = (mid[...] + jnp.transpose(result[...]) + vec_ref[5:6]).astype(BF)
    low_t = jnp.transpose(dlow)
    result[:LEAD] = dot(out_a[...], low_t)
    result[LEAD:] = dot(out_b_ref[...], low_t)
    o_perm[...] = jnp.transpose(result[...].astype(BF))

    def split_head(head, carry):
        do_ref[head] = dot(o_perm[...], head_pick(head)).astype(BF)
        return carry

    lax.fori_loop(0, HEADS, split_head, 0)


def middle(attn, first, slab, o, x, g, out_tail, vec, bias, tag):
    any_ = pl.BlockSpec(memory_space=pl.ANY)
    vmem = pl.BlockSpec(memory_space=pltpu.VMEM)
    sems = 3 * Gatherer.SEMS + 3
    turned = [(4, 2, 4, 2, 16, 256), (TAIL, 256)] * 3
    found = pl.pallas_call(
        middle_kernel,
        out_shape=tuple(
            [
                jax.ShapeDtypeStruct((256, D), BF),
                jax.ShapeDtypeStruct((HEADS, 256, LANES), BF),
                jax.ShapeDtypeStruct((256, D), F32),
                jax.ShapeDtypeStruct((256, D), BF),
                jax.ShapeDtypeStruct((8, D), F32),
                jax.ShapeDtypeStruct((1, FF_PAD), F32),
                jax.ShapeDtypeStruct((256, FF_PAD), BF),
                jax.ShapeDtypeStruct((256, FF_PAD), BF),
            ]
            + [jax.ShapeDtypeStruct(shape, BF) for shape in turned]
        ),
        in_specs=[any_] * 3 + [vmem] * 6,
        out_specs=(vmem,) * 14,
        scratch_shapes=[
            pltpu.VMEM((LEAD, D), BF),
            pltpu.VMEM((4, 2, 4, 2, 16, FIRST_TOTAL), BF),
            pltpu.VMEM((4, 2, 4, 2, 16, SECOND_TOTAL), BF),
            pltpu.VMEM((256, D), BF),
            pltpu.VMEM((256, D), F32),
            pltpu.VMEM((256, D), BF),
            pltpu.VMEM((D, 256), F32),
            pltpu.VMEM((D, 256), F32),
            pltpu.VMEM((FIRST_CHUNK // LANES, LEAD, LANES), F32),
            pltpu.VMEM((TAIL, 8 * FIRST_CHUNK), BF),
            pltpu.VMEM((1, FF_PAD), F32),
            pltpu.SemaphoreType.DMA((sems,)),
            pltpu.SemaphoreType.DMA((sems,)),
            pltpu.SemaphoreType.DMA((2,)),
        ],
        compiler_params=mesh_params(tag),
        name="middle",
    )(attn, first, slab, o, x, g, out_tail, vec, bias)
    return found[:8], found[12:14], found[8:10], found[10:12]


class Everyone:
    def __init__(self, place, core, slots, send, recv, base):
        self.place, self.core = place, core
        self.slots, self.send, self.recv, self.base = slots, send, recv, base

    def start(self, stage, value):
        if stage == 3:
            spot, targets = self.core, [(1, device_at(self.place, 1 - self.core))]
        else:
            axis = AXES[stage]
            spot = self.place[axis]
            targets = [
                (over, device_at(moved(self.place, axis, over), self.core)) for over in (2, 1, 3)
            ]
        self.slots[stage, spot] = value
        for over, device in targets:
            index = self.base + stage * 3 + over - 1
            slot = self.slots.at[stage, spot]
            remote(slot, slot, self.send.at[index], self.recv.at[index], device).start()

    def finish(self, stage):
        count = 2 if stage == 3 else 4
        for over in range(1, count):
            index = self.base + stage * 3 + over - 1
            spot = 1 - self.core if stage == 3 else cycle(self.place[AXES[stage]], 4 - over)
            slot = self.slots.at[stage, spot]
            remote(
                slot, slot, self.send.at[index], self.recv.at[index], device_at(self.place, self.core)
            ).wait_recv()
        total = self.slots[stage, 0]
        for spot in range(1, count):
            total = total + self.slots[stage, spot]
        return total

    def drain(self):
        for stage in range(4):
            for over in range(1, 2 if stage == 3 else 4):
                index = self.base + stage * 3 + over - 1
                slot = self.slots.at[stage, 0]
                remote(
                    slot,
                    slot,
                    self.send.at[index],
                    self.recv.at[index],
                    device_at(self.place, self.core),
                ).wait_send()


def finish_kernel(
    dheads,
    weight,
    dy,
    dpre,
    active,
    h_main,
    h_tail,
    o_main,
    o_tail,
    h2_main,
    h2_tail,
    g_main,
    g_tail,
    tail_ref,
    x_ref,
    dmid_ref,
    vec_ref,
    gvec_ref,
    gup_ref,
    tokens_ref,
    total_ref,
    share_ref,
    second_ref,
    dheads_all,
    weight_all,
    flat,
    flat_all,
    dy_all,
    dpre_all,
    active_all,
    h_main_all,
    h_tail_all,
    o_main_all,
    o_tail_all,
    h2_main_all,
    h2_tail_all,
    g_main_all,
    g_tail_all,
    extra,
    dh,
    vectors,
    slots,
    *rest,
):
    buffers, (send, recv, local) = rest[:-3], rest[-3:]
    place, core = here()
    red = Reducer(ATTN_WIDTHS, place, core, buffers[:18], share_ref, send, recv)
    base = 3 * Reducer.SEMS
    late = Reducer(SECOND_WIDTHS, place, core, buffers[18:], second_ref, send, recv, base)
    base = 2 * base
    twin = Twin(place, core, send, recv, base)
    late_twin = Twin(place, core, send, recv, base + 12)
    every = Everyone(place, core, slots, send, recv, base + 24)
    heads_in = pltpu.make_async_copy(dheads, dheads_all, local.at[0])
    heads_in.start()
    weight_in = pltpu.make_async_copy(weight.at[:, pl.ds(0, QKV)], weight_all, local.at[1])
    weight_in.start()
    greet(line_peers(place, core) + [device_at(place, 1 - core)])
    for source, target, axis in (
        (h2_main, h2_main_all, 5),
        (h2_tail, h2_tail_all, 1),
        (dpre.at[:, pl.ds(FIRST, SECOND)], dpre_all, 0),
        (g_main, g_main_all, 5),
        (g_tail, g_tail_all, 1),
        (active.at[:, pl.ds(FIRST, SECOND)], active_all, 0),
    ):
        late_twin.give(source, target, axis)
    for source, target, axis in (
        (h_main, h_main_all, 5),
        (h_tail, h_tail_all, 1),
        (o_main, o_main_all, 5),
        (o_tail, o_tail_all, 1),
        (dy, dy_all, 0),
    ):
        twin.give(source, target, axis)
    heads_in.wait()
    for head in range(HEADS):
        flat[:, PACK * head : PACK * head + PACK] = dheads_all[head, :, :PACK]
    twin.give(flat, flat_all, 0)

    def make_all(reducer, maker):
        maker.pack_tail()
        for part in range(3):
            maker.make(part, 2)
        reducer.far_out()

        def others(index, carry):
            ahead = cycle(index, 3)
            for part in range(3):
                maker.make(part, ahead)
            return carry

        lax.fori_loop(0, 3, others, 0)

    late_twin.ready()
    make_all(
        late,
        Maker(
            late,
            [((h2_main_all, h2_tail_all), dpre_all), ((g_main_all, g_tail_all), active_all)],
            extra.at[pl.ds(0, SECOND_CHUNK // LANES)],
            SECOND_CHUNK,
        ),
    )
    twin.ready()
    make_all(
        red,
        Maker(
            red,
            [((h_main_all, h_tail_all), flat_all), ((o_main_all, o_tail_all), dy_all)],
            extra,
            ATTN_CHUNK,
        ),
    )
    for spot in range(4):
        late.pass_on(spot)
    dh[...] = jnp.zeros_like(dh)
    vectors[...] = jnp.zeros((VEC_ROWS, D), F32)
    vectors[2:6] = gvec_ref[:4]
    for row in range(4):
        span = slice(row * D, min((row + 1) * D, FF_PAD))
        vectors[VEC_UP + row : VEC_UP + row + 1, : span.stop - span.start] = gup_ref[:, span]
    weight_in.wait()

    for row in range(3):

        def columns(index, carry):
            span = lanes(row * D + index * 384, 384)
            value = flat[:, span]
            vectors[VEC_QKV + row : VEC_QKV + row + 1, lanes(index * 384, 384)] = column_total(
                value.astype(F32)
            )
            value_t = jnp.transpose(value)
            dh[:LEAD] += dot(weight_all[:, span], value_t)
            dh[LEAD:] += dot(tail_ref[:, span], value_t)
            return carry

        lax.fori_loop(0, 3, columns, 0)
    for spot in range(4):
        red.pass_on(spot)
    unit, rate = normal(x_ref[...].astype(F32))
    grad = jnp.transpose(dh[...])
    vectors[0:1] = column_total(grad * unit)
    vectors[1:2] = column_total(grad)
    every.start(0, vectors[...])
    total = dmid_ref[...] + normal_back(unit, rate, vec_ref[0:1], grad)
    tokens_ref[...] = total.astype(BF)
    for over in (2, 1, 3):
        late.gather_side(over, False)
    every.start(1, every.finish(0))
    late.gather_side(0, True)
    for over in (2, 1, 3):
        red.gather_side(over, False)
    every.start(2, every.finish(1))
    red.gather_side(0, True)
    late.line_up()
    every.start(3, every.finish(2))
    red.line_up()
    late.share()
    total_ref[...] = every.finish(3)
    red.share()
    late.close()
    red.close()
    twin.drain()
    late_twin.drain()
    every.drain()


def finish(dheads, weight, dy, dpre, active, turned, tail, x, dmid, vec, gvec, gup, tag):
    any_ = pl.BlockSpec(memory_space=pl.ANY)
    vmem = pl.BlockSpec(memory_space=pltpu.VMEM)
    sems = 6 * Reducer.SEMS + 24 + 12
    rows = [pltpu.VMEM((4, 2, 4, 2, 16, 512), BF), pltpu.VMEM((TAIL, 512), BF)]
    return pl.pallas_call(
        finish_kernel,
        out_shape=(
            jax.ShapeDtypeStruct((256, D), BF),
            jax.ShapeDtypeStruct((VEC_ROWS, D), F32),
            jax.ShapeDtypeStruct((16, ATTN_TOTAL), BF),
            jax.ShapeDtypeStruct((16, SECOND_TOTAL), BF),
        ),
        in_specs=[any_] * 13 + [vmem] * 6,
        out_specs=(vmem,) * 4,
        scratch_shapes=[
            pltpu.VMEM((HEADS, 256, WIDE), BF),
            pltpu.VMEM((LEAD, QKV), BF),
            pltpu.VMEM((256, QKV), BF),
            pltpu.VMEM((512, QKV), BF),
            pltpu.VMEM((512, D), BF),
            pltpu.VMEM((512, SECOND), BF),
            pltpu.VMEM((512, SECOND), BF),
        ]
        + rows * 4
        + [
            pltpu.VMEM((ATTN_CHUNK // LANES, LEAD, LANES), F32),
            pltpu.VMEM((D, 256), F32),
            pltpu.VMEM((VEC_ROWS, D), F32),
            pltpu.VMEM((4, 4, VEC_ROWS, D), F32),
        ]
        + Reducer.scratch(ATTN_WIDTHS)
        + Reducer.scratch(SECOND_WIDTHS)
        + [
            pltpu.SemaphoreType.DMA((sems,)),
            pltpu.SemaphoreType.DMA((sems,)),
            pltpu.SemaphoreType.DMA((2,)),
        ],
        compiler_params=mesh_params(tag),
        name="finish",
    )(dheads, weight, dy, dpre, active, *turned, tail, x, dmid, vec, gvec, gup)


def close_kernel(
    totals_ref,
    attn_ref,
    first_ref,
    second_ref,
    mixed_in,
    tokens_in,
    mixed_ref,
    tokens_ref,
    query_ref,
    key_ref,
    value_ref,
    out_ref,
    up_ref,
    down_ref,
    gain1_ref,
    bias1_ref,
    gain2_ref,
    bias2_ref,
    bias_out_ref,
    bias_down_ref,
    bias_query_ref,
    bias_value_ref,
    bias_up_ref,
    attn,
    first,
    second,
    vec,
):
    def unpack(share, full, main, chunk):
        full[0:16, :] = share[:, :main].astype(F32)
        rest = share[:, main : main + chunk].astype(F32)
        for row in range(2):
            for index in range(8):
                size = min(main - index * chunk, chunk)
                if size > 0:
                    start = index * chunk
                    spot = row * 8 + index
                    full[16 + row : 17 + row, start : start + size] = rest[
                        spot : spot + 1, :size
                    ]

    unpack(attn_ref, attn, ATTN_MAIN, ATTN_CHUNK)
    unpack(first_ref, first, 2 * FIRST, FIRST_CHUNK)
    unpack(second_ref, second, 2 * SECOND, SECOND_CHUNK)
    for head in range(HEADS):
        span = slice(head * HEAD_DIM, (head + 1) * HEAD_DIM)
        for index, ref in enumerate((key_ref, query_ref, value_ref)):
            start = head * PACK + index * HEAD_DIM
            ref[:, span] = attn[:18, start : start + HEAD_DIM]
    low = attn[:, QKV:ATTN_MAIN].astype(BF)

    def restore(index, carry):
        columns = lanes(index * LANES, LANES)
        matrix = unmix(index)
        out_ref[:, columns] = dot(low, matrix)[:18]
        mixed_ref[:, columns] = dot(mixed_in[...], matrix).astype(BF)
        tokens_ref[:, columns] = dot(tokens_in[...], matrix).astype(BF)
        vec[0:8, columns] = jnp.dot(
            totals_ref[0:8, :],
            matrix.astype(F32),
            precision=lax.Precision.HIGHEST,
            preferred_element_type=F32,
        )
        return carry

    lax.fori_loop(0, 9, restore, 0)
    lines = (gain1_ref, bias1_ref, gain2_ref, bias2_ref, bias_out_ref, bias_down_ref)
    for index, ref in enumerate(lines):
        ref[...] = vec[index : index + 1, :D].reshape(D)
    for row in range(3):
        vec[8:9, row * D : (row + 1) * D] = totals_ref[VEC_QKV + row : VEC_QKV + row + 1, :]
    for head in range(HEADS):
        span = slice(head * HEAD_DIM, (head + 1) * HEAD_DIM)
        for index, row in ((1, 9), (2, 10)):
            start = head * PACK + index * HEAD_DIM
            vec[row : row + 1, span] = vec[8:9, start : start + HEAD_DIM]
    bias_query_ref[...] = vec[9:10, :D].reshape(D)
    bias_value_ref[...] = vec[10:11, :D].reshape(D)
    for row in range(4):
        size = min(FF - row * D, D)
        vec[11:12, row * D : row * D + size] = totals_ref[
            VEC_UP + row : VEC_UP + row + 1, :size
        ]
    bias_up_ref[...] = vec[11:12, :FF].reshape(FF)
    up_ref[:, :FIRST] = first[:18, :FIRST]
    up_ref[:, FIRST:] = second[:18, : FF - FIRST]
    down_ref[:, :FIRST] = first[:18, FIRST : 2 * FIRST]
    down_ref[:, FIRST:] = second[:18, SECOND : SECOND + FF - FIRST]


def close_layer(totals, attn, first, second, mixed, tokens):
    line = jax.ShapeDtypeStruct((D,), F32)
    square = jax.ShapeDtypeStruct((18, D), F32)
    return pl.pallas_call(
        close_kernel,
        out_shape=(
            jax.ShapeDtypeStruct((256, D), BF),
            jax.ShapeDtypeStruct((256, D), BF),
            square,
            square,
            square,
            square,
            jax.ShapeDtypeStruct((18, FF), F32),
            jax.ShapeDtypeStruct((18, FF), F32),
            *([line] * 8),
            jax.ShapeDtypeStruct((FF,), F32),
        ),
        scratch_shapes=[
            pltpu.VMEM((24, ATTN_MAIN), F32),
            pltpu.VMEM((24, 2 * FIRST), F32),
            pltpu.VMEM((24, 2 * SECOND), F32),
            pltpu.VMEM((16, 4 * D), F32),
        ],
        compiler_params=params(),
        name="close_layer",
    )(totals, attn, first, second, mixed, tokens)


def pack_slab(weight, chunk, total):
    width = weight.shape[1]
    rest = jnp.pad(weight[16:], ((0, 0), (0, 8 * chunk - width))).reshape(16, chunk)
    return jnp.concatenate(
        [weight[:16], rest, jnp.zeros((16, total - width - chunk), weight.dtype)], axis=1
    )


def by_head(key, query, value):
    rows = key.shape[0]
    parts = [item.reshape(rows, HEADS, 1, HEAD_DIM) for item in (key, query, value)]
    return jnp.concatenate(parts, axis=2).reshape(rows, QKV)


def mixing():
    return onehot(iota((D, D), 0) == origin(iota((D, D), 1)))


def body(
    tokens,
    picture,
    cotangent,
    ln1_gain,
    ln1_bias,
    w_query,
    b_query,
    w_key,
    w_value,
    b_value,
    w_out,
    b_out,
    ln2_gain,
    ln2_bias,
    w_fc1,
    b_fc1,
    w_fc2,
    b_fc2,
):
    mix = mixing()
    out_cols = dot(w_out, mix).astype(BF)
    attn_slab = pack_slab(
        jnp.concatenate([by_head(w_key, w_query, w_value), out_cols], axis=1),
        ATTN_CHUNK,
        ATTN_TOTAL,
    )
    gap = ((0, 0), (0, FF_PAD - FF))
    up, down = jnp.pad(w_fc1, gap), jnp.pad(w_fc2.T, gap)
    first_slab = pack_slab(
        jnp.concatenate([up[:, :FIRST], down[:, :FIRST]], axis=1), FIRST_CHUNK, FIRST_TOTAL
    )
    second_slab = pack_slab(
        jnp.concatenate([up[:, FIRST:], down[:, FIRST:]], axis=1), SECOND_CHUNK, SECOND_TOTAL
    )
    lines = (ln1_gain, ln1_bias, ln2_gain, ln2_bias, b_out, b_fc2, b_query, b_value)
    heads, x, g, h_main, h_tail, attn_tail, out_tail, vec, attn = open_layer(
        attn_slab, tokens.reshape(256, D), cotangent.reshape(256, D), lines, 0
    )
    attn = attn.reshape(LEAD, ATTN_TOTAL)
    packed, keep, o, first = attend_gather(heads, first_slab, picture, 1)
    (mixed, go, dmid, dy, gvec2, gbias1, dpre, active), o_turned, h_turned, g_turned = middle(
        attn, first, second_slab, o, x, g, out_tail, vec, b_fc1, 2
    )
    first_share, dheads = attend_back_reduce(
        go, dpre, active, (*h_turned, *g_turned), packed, keep, picture, 3
    )
    gtokens, totals, attn_share, second_share = finish(
        dheads,
        attn,
        dy,
        dpre,
        active,
        (h_main, h_tail, *o_turned, *h_turned, *g_turned),
        attn_tail,
        x,
        dmid,
        vec,
        gvec2,
        gbias1,
        4,
    )
    (
        mixed,
        gtokens,
        grad_query,
        grad_key,
        grad_value,
        grad_out,
        grad_up,
        grad_down,
        grad_gain1,
        grad_bias1,
        grad_gain2,
        grad_bias2,
        grad_b_out,
        grad_b_fc2,
        grad_b_query,
        grad_b_value,
        grad_b_fc1,
    ) = close_layer(totals, attn_share, first_share, second_share, mixed, gtokens)
    return (
        mixed.reshape(2, 128, D),
        gtokens.reshape(2, 128, D),
        grad_gain1,
        grad_bias1,
        grad_query,
        grad_b_query,
        grad_key,
        grad_value,
        grad_b_value,
        grad_out,
        grad_b_out,
        grad_gain2,
        grad_bias2,
        grad_up,
        grad_b_fc1,
        grad_down.T,
        grad_b_fc2,
    )


def solution(mesh):
    placed = (
        P(None, ("fsdp", "rep"), None),
        P(),
        P(None, ("fsdp", "rep"), None),
        P(),
        P(),
        P("fsdp", None),
        P(),
        P("fsdp", None),
        P("fsdp", None),
        P(),
        P("fsdp", None),
        P(),
        P(),
        P(),
        P("fsdp", None),
        P(),
        P(None, "fsdp"),
        P(),
    )
    return jax.shard_map(
        body,
        mesh=mesh,
        in_specs=placed,
        out_specs=(
            P(None, ("fsdp", "rep"), None),
            P(None, ("fsdp", "rep"), None),
            P(),
            P(),
            P("fsdp", None),
            P(),
            P("fsdp", None),
            P("fsdp", None),
            P(),
            P("fsdp", None),
            P(),
            P(),
            P(),
            P("fsdp", None),
            P(),
            P(None, "fsdp"),
            P(),
        ),
        check_vma=False,
    )
```

profile of v0, /device:TPU:0, one launch (start us, length us, event | category | flops | bytes accessed | tf_op | source)
XLA Modules:
  0.0 334.9 jit_solution(5196206641788087721)
XLA Ops:
  0.7 0.0 copy-start
  0.7 0.8 copy-done
  1.5 0.0 copy-start.1
  1.5 0.0 copy-start.2
  1.5 0.0 copy-start.3
  1.5 0.0 copy-start.4
  1.5 0.0 copy-start.5
  1.5 0.5 fusion.5
  2.0 0.4 copy-done.1
  2.4 0.1 copy-done.2
  2.6 0.0 copy-done.3
  2.6 0.3 reshape.83
  2.9 0.0 copy-done.4
  2.9 0.3 reshape.82
  3.2 0.0 copy-done.5
  3.2 0.3 reshape.84
  3.5 0.6 pad_maximum_fusion
  4.1 0.4 reshape.73
  4.5 0.8 maximum_maximum_fusion.1
  5.4 0.7 pad_maximum_fusion.1.slab
  6.1 49.5 %open_layer.1 = (bf16[16,256,256]{2,1,0:T(8,128)(2,1)}, bf16[256,1152]{1,0:T(8,128)(2,1)}, bf16[256,1152]{1,0:T(8,128)(2,1)}, bf16[4,2,4,2,16,256]{5,4,3,2,1,0:T...) custom-call(bf16[16,5376]{1,0:T(8,128)(2,1)} %get-tuple-element.118., ...), custom_call_target="tpu_custom_call" | custom-call | tf_op jit(solution)/shard_map/open_layer/pallas_call | solution.py:1013
  55.5 68.0 %attend_gather.1 = (bf16[16,256,256]{2,1,0:T(8,128)(2,1)}, f32[2,2048,128]{2,1,0:T(8,128)}, bf16[16,256,128]{2,1,0:T(8,128)(2,1)}, bf16[4,2,4,2,16,5376]{5,4,3,2,1,0:T(8,128)(2,1)}) custom-call(bf16[16,256,256]{2,1,0:T(8,128)(2,1)} %get-tuple-element.68.heads, bf16[16,5376]{1,0:T(8,128)(2,1)} %get-tuple-element.117.slab, s32[2,16384]{1,0:T(2,128)} %picture.3), custom_call_target="tpu_custom_call" | custom-call | tf_op jit(solution)/shard_map/attend_gather/pallas_call | solution.py:1167
  123.6 52.2 %middle.1 = (bf16[256,1152]{1,0:T(8,128)(2,1)}, bf16[16,256,128]{2,1,0:T(8,128)(2,1)}, f32[256,1152]{1,0:T(8,128)}, bf16[256,1152]{1,0:T(8,128)(2,1)}, f32[8,115...) custom-call(bf16[1024,5376]{1,0:T(8,128)(2,1)} %bitcast.10, ...), custom_call_target="tpu_custom_call" | custom-call | tf_op jit(solution)/shard_map/middle/pallas_call | solution.py:1365
  175.8 78.2 %attend_back_reduce.1 = (bf16[16,5376]{1,0:T(8,128)(2,1)}, bf16[16,256,256]{2,1,0:T(8,128)(2,1)}) custom-call(bf16[16,256,128]{2,1,0:T(8,128)(2,1)} %get-tuple-element.75.go, bf16[256,4352]{1,0:T(8,128)(2,1)} %get-tuple-element.76.dpre, bf16[256,4352]{1,0:T(8,128)(2,1)} %get-tuple-element.77.active, ...), custom_call_target="tpu_custom_call" | custom-call | tf_op jit(solution)/shard_map/attend_back_reduce/pallas_call | solution.py:858
  253.9 69.5 %finish.1 = (bf16[256,1152]{1,0:T(8,128)(2,1)}, f32[16,1152]{1,0:T(8,128)}, bf16[16,5376]{1,0:T(8,128)(2,1)}, bf16[16,4608]{1,0:T(8,128)(2,1)}) custom-call(bf16[16,256,256]{2,1,0:T(8,128)(2,1)} %get-tuple-element.84.dheads, bf16[1024,5376]{1,0:T(8,128)(2,1)} %bitcast.11, bf16[256,1152]{1,0:T(8,128)(2,1)} %get-tuple-element.85.dy, ...), custom_call_target="tpu_custom_call" | custom-call | tf_op jit(solution)/shard_map/finish/pallas_call | solution.py:1626
  323.5 11.2 %close_layer.1 = (bf16[256,1152]{1,0:T(8,128)(2,1)}, bf16[256,1152]{1,0:T(8,128)(2,1)}, f32[18,1152]{1,0:T(8,128)}, f32[18,1152]{1,0:T(8,128)}, f32[18,1152]{1,0...) custom-call(f32[16,1152]{1,0:T(8,128)} %get-tuple-element.94.totals_, ...), custom_call_target="tpu_custom_call" | custom-call | tf_op jit(solution)/shard_map/close_layer/pallas_call | solution.py:1758
  (16 shorter events, 0.2 us)
Async XLA Ops:
  0.7 0.8 copy-start
  1.5 0.9 copy-start.1
  1.5 1.0 copy-start.2
  1.5 1.1 copy-start.3
  1.5 1.4 copy-start.4
  1.5 1.7 copy-start.5
where the time goes:
time: 340 us; the launch traced here: 335 us
  Pallas kernels  329 us (97%)
    pallas_call x1, Pallas kernels, attend_back_reduce(): pl.pallas_call(back_kernel, out_shape=(jax.ShapeDtypeStruct((16, FIRST_TO...  78.2 us
    pallas_call x1, Pallas kernels, finish(): pl.pallas_call(finish_kernel, out_shape=(jax.ShapeDtypeStruct((256, D), B...  69.5 us
    pallas_call x1, Pallas kernels, attend_gather(): pl.pallas_call(attend_kernel, out_shape=(jax.ShapeDtypeStruct((16, 256, W...  68 us
    pallas_call x1, Pallas kernels, middle(): pl.pallas_call(middle_kernel, out_shape=tuple([jax.ShapeDtypeStruct((256,...  52.2 us
    pallas_call x1, Pallas kernels, open_layer(): pl.pallas_call(open_kernel, out_shape=(jax.ShapeDtypeStruct((HEADS, 256,...  49.5 us
    pallas_call x1, Pallas kernels, close_layer(): pl.pallas_call(close_kernel, out_shape=(jax.ShapeDtypeStruct((256, D), BF...  11.2 us

commit v1 on v0

--- a/solution.py
+++ b/solution.py
@@ -394,29 +394,16 @@
                 :, tile * LANES : (tile + 1) * LANES
             ]
 
-    def rows(self, ref, part, ahead):
-        place, core = self.red.place, self.red.core
-        three = ORDERS[part][2]
-        spot = cycle(place[three], ahead)
+    def rows(self, ref):
+        core = self.red.core
         if len(ref.shape) == 2:
-            if three == "z":
-                groups = [outer * 8 + spot * 2 + core for outer in range(8)]
-            elif three == "x":
-                groups = [spot * 16 + inner * 2 + core for inner in range(8)]
-            else:
-                high = lax.div(spot, 2) * 8
-                groups = [x * 16 + high + z * 2 + core for x in range(4) for z in range(4)]
-            found = [ref[pl.ds(pl.multiple_of(group * 16, 16), 16)] for group in groups]
-            return jnp.concatenate(found, axis=0)
-        if three == "z":
-            value = ref[:, :, spot, core]
-        elif three == "x":
-            value = ref[spot, :, :, core]
-        else:
-            value = ref[:, lax.div(spot, 2), :, core]
-        return value.reshape(-1, ref.shape[-1])
-
-    def columns(self, part, half, ahead):
+            groups = [
+                ref[pl.ds(pl.multiple_of((2 * index + core) * 16, 16), 16)] for index in range(32)
+            ]
+            return jnp.concatenate(groups, axis=0)
+        return ref[:, :, :, core].reshape(512, ref.shape[-1])
+
+    def columns(self, part, half):
         width = self.red.widths[part]
         low = 2 * sum(self.red.widths[:part]) + half * width
         high = low + width
@@ -426,41 +413,49 @@
             last = first + right.shape[1]
             a, b = max(low, first), min(high, last)
             if a < b:
-                left = self.rows(turned[0], part, ahead)
+                left = self.rows(turned[0])
                 found.append(dot(left, right[:, a - first : b - first]).astype(BF))
             first = last
         a, b = max(low, first), min(high, first + self.chunk)
         if a < b:
             for tile in range((a - first) // LANES, (b - first) // LANES):
-                found.append(self.rows(self.extra.at[tile], part, ahead).astype(BF))
+                found.append(self.rows(self.extra.at[tile]).astype(BF))
         a = max(low, first + self.chunk)
         if a < high:
-            found.append(jnp.zeros((found[0].shape[0], high - a), BF))
+            found.append(jnp.zeros((512, high - a), BF))
         return found[0] if len(found) == 1 else jnp.concatenate(found, axis=1)
 
-    def make(self, part, ahead):
+    def make(self, part):
         red, width = self.red, self.red.widths[part]
         acc = red.acc[part]
         three = ORDERS[part][2]
-        if three == "z":
-            for half in range(2):
-                value = self.columns(part, half, ahead).reshape(4, 2, 16, width)
+        own = red.place[three]
+
+        def ahead(spot):
+            return cycle(spot + 4 - own, 0)
+
+        for half in range(2):
+            value = self.columns(part, half).reshape(4, 2, 4, 16, width)
+            if three == "z":
+                for spot in range(4):
+                    for high in range(2):
+                        acc[ahead(spot), 2 * high + half] = value[:, high, spot]
+            elif three == "x":
+                for spot in range(4):
+                    for z in range(4):
+                        acc[ahead(spot), z, :, :, half * width : (half + 1) * width] = value[
+                            spot, :, z
+                        ]
+            else:
                 for high in range(2):
-                    acc[ahead, 2 * high + half] = value[:, high]
-        elif three == "x":
-            for half in range(2):
-                value = self.columns(part, half, ahead).reshape(2, 4, 16, width)
-                for spot in range(4):
-                    acc[ahead, spot, :, :, half * width : (half + 1) * width] = value[:, spot]
-        else:
-            low = lax.rem(cycle(red.place["y"], ahead), 2)
-            for half in range(2):
-
-                @pl.when(low == half)
-                def _(half=half):
-                    value = self.columns(part, half, ahead).reshape(4, 4, 16, width)
-                    for spot in range(4):
-                        acc[ahead, spot] = value[spot]
+                    for x in range(4):
+                        acc[ahead(2 * high + half), x] = value[x, high]
+
+    def run(self):
+        self.pack_tail()
+        for part in range(3):
+            self.make(part)
+        self.red.far_out()
 
 
 SWAP_ORDER = (9, 11, 5, 13, 7, 15, 1, 3, 8, 10, 4, 12, 6, 14, 2)
@@ -566,16 +561,16 @@
 MLP_TOTAL = 9984
 ATTN_WIDTHS = (896, 896, 896)
 MLP_WIDTHS = (1664, 1664, 1664)
-FIRST = 2304
-FIRST_CHUNK = 640
-FIRST_TOTAL = 5376
-FIRST_WIDTHS = (896, 896, 896)
+FIRST = 3072
+FIRST_CHUNK = 768
+FIRST_TOTAL = 6912
+FIRST_WIDTHS = (1152, 1152, 1152)
 FIRST_STEP = 768
 SECOND = FF_PAD - FIRST
-SECOND_CHUNK = 512
-SECOND_TOTAL = 4608
-SECOND_WIDTHS = (768, 768, 768)
-SECOND_STEP = 512
+SECOND_CHUNK = 384
+SECOND_TOTAL = 3072
+SECOND_WIDTHS = (512, 512, 512)
+SECOND_STEP = 640
 LOG2E = 1.4426950408889634
 QUERIES = 512
 KEYS = 512
@@ -624,6 +619,14 @@
     return rate * (inner - first - unit * second)
 
 
+def exact_parts(values):
+    high = values.astype(BF)
+    rest = values - high.astype(F32)
+    middle_part = rest.astype(BF)
+    low = (rest - middle_part.astype(F32)).astype(BF)
+    return jnp.concatenate([high, middle_part, low], axis=0)
+
+
 def column_total(values):
     return jnp.sum(values, axis=0, keepdims=True)
 
@@ -636,20 +639,23 @@
     return pltpu.CompilerParams(vmem_limit_bytes=limit << 20)
 
 
-def head_place(head):
-    spot = iota((LANES, D), 0) - VALUE_LANE
-    inside = (spot >= 0) & (spot < HEAD_DIM)
-    return onehot(inside & (origin(iota((LANES, D), 1)) == HEAD_DIM * head + spot))
-
-
-def head_pick(head):
-    spot = iota((D, LANES), 1) - VALUE_LANE
-    inside = (spot >= 0) & (spot < HEAD_DIM)
-    return onehot(inside & (origin(iota((D, LANES), 0)) == HEAD_DIM * head + spot))
-
-
-def unmix(value):
-    return onehot(origin(iota((D, LANES), 0)) == value * LANES + iota((D, LANES), 1))
+PERMUTED = np.concatenate(
+    [np.arange(64)[:, None] * 18 + np.arange(16), np.arange(64)[:, None] * 18 + [16, 17]], axis=1
+)
+PERMUTED = np.concatenate([PERMUTED[:, :16].reshape(-1), PERMUTED[:, 16:].reshape(-1)])
+
+
+def mix_matrix():
+    matrix = np.zeros((D, D), np.float32)
+    matrix[PERMUTED, np.arange(D)] = 1.0
+    return matrix
+
+
+def place_matrix():
+    matrix = np.zeros((HEADS, LANES, D), np.float32)
+    mixed = mix_matrix().reshape(HEADS, HEAD_DIM, D)
+    matrix[:, VALUE_LANE : VALUE_LANE + HEAD_DIM] = mixed
+    return matrix.reshape(HEADS * LANES, D)
 
 
 def mesh_params(tag, limit=62):
@@ -756,18 +762,7 @@
     for micro in range(2):
         row_ref[micro] = found[micro : micro + 1].astype(F32)
     twin.ready()
-    maker.pack_tail()
-    for part in range(3):
-        maker.make(part, 2)
-    red.far_out()
-
-    def others(index, carry):
-        ahead = cycle(index, 3)
-        for part in range(3):
-            maker.make(part, ahead)
-        return carry
-
-    lax.fori_loop(0, 3, others, 0)
+    maker.run()
     swap_in.finish()
 
     def block(step, carry):
@@ -787,37 +782,44 @@
 
         rows = pl.ds(pl.multiple_of(index * QUERIES, QUERIES), QUERIES)
         groups = pl.ds(index * (QUERIES // 128), QUERIES // 128)
-        query = queries[rows, :]
-        back = go_all[groups, tokens, :].reshape(QUERIES, LANES)
-        mine = row_ref[row, :, lanes(index * QUERIES, QUERIES)]
-        kept = keep_ref[row, rows, :]
-        inner = jnp.sum(back.astype(F32) * kept, axis=1, keepdims=True)
-        lane = iota((QUERIES, LANES), 1)
-        stats = jnp.transpose(jnp.where(lane == 0, kept, inner))
-        logsum = stats[0:1]
-        inner = stats[1:2]
-        total = jnp.zeros((QUERIES, LANES), F32)
-        for part in range(ROW // KEYS):
-            span = slice(part * KEYS, (part + 1) * KEYS)
-            blocks = slice(part * KEYS // 128, (part + 1) * KEYS // 128)
-            value = packed_ref[blocks, tokens, LANES:].reshape(KEYS, LANES)
-            allowed = jnp.concatenate([ids[span, :]] * (QUERIES // LANES), axis=1)
-            score = dot_nt(keys[span, :], query) * (SCALE * LOG2E) - logsum
-            prob = jnp.exp2(jnp.where(allowed == mine, score, NEG))
-            grad = (prob * (dot_nt(value, back) - inner)).astype(BF)
-            dvalues[span, :] += dot(prob.astype(BF), back)
-            dkeys[span, :] += dot(grad, query)
-            total = total + dot_tn(grad, keys[span, :])
-        total = total * SCALE
-        moved_q = jnp.concatenate(
-            [
-                jnp.zeros((QUERIES, HEAD_DIM), F32),
-                total[:, :HEAD_DIM],
-                jnp.zeros((QUERIES, WIDE - 2 * HEAD_DIM), F32),
-            ],
-            axis=1,
-        )
-        grads[groups, tokens, :] = moved_q.astype(BF).reshape(QUERIES // 128, 128, WIDE)
+
+        def scan(count):
+            start = jnp.where(index < 2, 0, BLOCKS - count)
+            query = queries[rows, :]
+            back = go_all[groups, tokens, :].reshape(QUERIES, LANES)
+            mine = row_ref[row, :, lanes(index * QUERIES, QUERIES)]
+            kept = keep_ref[row, rows, :]
+            inner = jnp.sum(back.astype(F32) * kept, axis=1, keepdims=True)
+            lane = iota((QUERIES, LANES), 1)
+            stats = jnp.transpose(jnp.where(lane == 0, kept, inner))
+            logsum = stats[0:1]
+            inner = stats[1:2]
+            total = jnp.zeros((QUERIES, LANES), F32)
+            for part in range(count):
+                span = pl.ds(pl.multiple_of((start + part) * KEYS, KEYS), KEYS)
+                blocks = pl.ds((start + part) * (KEYS // 128), KEYS // 128)
+                value = packed_ref[blocks, tokens, LANES:].reshape(KEYS, LANES)
+                allowed = jnp.concatenate([ids[span, :]] * (QUERIES // LANES), axis=1)
+                score = dot_nt(keys[span, :], query) * (SCALE * LOG2E) - logsum
+                prob = jnp.exp2(jnp.where(allowed == mine, score, NEG))
+                grad = (prob * (dot_nt(value, back) - inner)).astype(BF)
+                dvalues[span, :] += dot(prob.astype(BF), back)
+                dkeys[span, :] += dot(grad, query)
+                total = total + dot_tn(grad, keys[span, :])
+            total = total * SCALE
+            moved_q = jnp.concatenate(
+                [
+                    jnp.zeros((QUERIES, HEAD_DIM), F32),
+                    total[:, :HEAD_DIM],
+                    jnp.zeros((QUERIES, WIDE - 2 * HEAD_DIM), F32),
+                ],
+                axis=1,
+            )
+            grads[groups, tokens, :] = moved_q.astype(BF).reshape(QUERIES // 128, 128, WIDE)
+
+        edge = (index == 0) | (index == BLOCKS - 1)
+        pl.when(edge)(functools.partial(scan, 3))
+        pl.when(jnp.logical_not(edge))(functools.partial(scan, 4))
 
         @pl.when(index == BLOCKS - 1)
         def _():
@@ -906,22 +908,48 @@
             tail[:, start : start + LANES] = picked.astype(BF)
 
 
-def open_kernel(
+def column_ids(row_ids):
+    size = row_ids.shape[1]
+    return jnp.transpose(jnp.broadcast_to(row_ids, (LANES, size)))
+
+
+def fetch_ids(picture, found, sem):
+    start = pl.multiple_of(lax.div(lax.axis_index("fsdp"), 8) * ROW, ROW)
+    return pltpu.make_async_copy(picture.at[:, pl.ds(start, ROW)], found, sem)
+
+
+def split_packed(packed, keys, queries):
+    lane = iota((ROW, LANES), 1)
+    zero = jnp.zeros((ROW, LANES), BF)
+    keys[...] = jnp.where(lane < HEAD_DIM, packed[:, :LANES], zero)
+    queries[...] = jnp.concatenate(
+        [packed[:, HEAD_DIM : 2 * HEAD_DIM], jnp.zeros((ROW, LANES - HEAD_DIM), BF)], axis=1
+    )
+
+
+def swap_only(swapper):
+    return [swapper.device(swapper.member(k)) for k in range(1, 16) if k not in (1, 4, 8, 12)]
+
+
+def front_kernel(
     slab,
+    first_slab,
+    picture,
     tokens_ref,
     cotangent_ref,
     *refs,
 ):
     lines, rest = refs[:8], refs[8:]
-    run_open(slab, tokens_ref, cotangent_ref, lines, *rest)
-
-
-def run_open(
+    run_front(slab, first_slab, picture, tokens_ref, cotangent_ref, lines, *rest)
+
+
+def run_front(
     slab,
+    first_slab,
+    picture,
     tokens_ref,
     cotangent_ref,
     lines,
-    heads_ref,
     x_ref,
     g_ref,
     h_main_ref,
@@ -929,149 +957,19 @@
     tail_ref,
     out_tail_ref,
     mixed_vec_ref,
+    packed_ref,
+    keep_ref,
+    o_all,
     weight_out,
+    first_out,
     full,
     low,
     flat,
     wide,
     tail,
     vec_ref,
-    send,
-    recv,
-    local,
-):
-    place, core = here()
-    red = Gatherer(ATTN_WIDTHS, place, core, slab, full, send, recv, 0)
-    greet(line_peers(place, core) + [device_at(place, 1 - core)])
-    red.start()
-    for index, line in enumerate(lines):
-        vec_ref[index : index + 1, :] = line[...].reshape(1, D)
-
-    def mix(index, carry):
-        columns = lanes(index * LANES, LANES)
-        column = onehot(iota((D, LANES), 0) == origin(index * LANES + iota((D, LANES), 1)))
-        x_ref[:, columns] = dot(tokens_ref[...], column).astype(BF)
-        g_ref[:, columns] = dot(cotangent_ref[...], column).astype(BF)
-        mixed_vec_ref[:, columns] = jnp.dot(
-            vec_ref[...],
-            column.astype(F32),
-            precision=lax.Precision.HIGHEST,
-            preferred_element_type=F32,
-        )
-        return carry
-
-    lax.fori_loop(0, 9, mix, 0)
-    red.second()
-    unit, _ = normal(x_ref[...].astype(F32))
-    low[...] = (unit * mixed_vec_ref[0:1] + mixed_vec_ref[1:2]).astype(BF)
-    for steps in (1, 2, 3):
-        red.third(steps)
-    turned = jnp.transpose(low[...])
-    h_main_ref[...] = turned[:LEAD].reshape(4, 2, 4, 2, 16, 256)
-    h_tail_ref[...] = turned[LEAD:]
-    for steps in range(4):
-        red.fourth(steps)
-    for steps in range(4):
-        red.fifth(steps)
-    red.close()
-    leave = pltpu.make_async_copy(full, weight_out, local.at[0])
-    leave.start()
-
-    def packed(tile):
-        start = ATTN_MAIN + tile * LANES
-        return full[:, :, :, :, :, start : start + LANES].reshape(LEAD, LANES)
-
-    spread_tail(packed, ATTN_CHUNK, wide, tail)
-    tail_ref[...] = tail[:, :QKV]
-    out_tail_ref[...] = tail[:, QKV:ATTN_MAIN]
-
-    def columns(index, carry):
-        span = lanes(index * 384, 384)
-        weight = full[:, :, :, :, :, span].reshape(LEAD, 384)
-        flat[:, span] = dot(low[:, :LEAD], weight) + dot(low[:, LEAD:], tail[:, span])
-        return carry
-
-    lax.fori_loop(0, QKV // 384, columns, 0)
-    for head in range(HEADS):
-        span = slice(head * HEAD_DIM, (head + 1) * HEAD_DIM)
-        bias = jnp.concatenate(
-            [jnp.zeros((1, HEAD_DIM), F32), vec_ref[6:7, span], vec_ref[7:8, span]], axis=1
-        )
-        block = flat[:, PACK * head : PACK * head + PACK] + bias
-        heads_ref[head] = jnp.concatenate(
-            [block, jnp.zeros((256, WIDE - PACK), F32)], axis=1
-        ).astype(BF)
-    red.drain()
-    leave.wait()
-
-
-def open_layer(slab, tokens, cotangent, lines, tag):
-    any_ = pl.BlockSpec(memory_space=pl.ANY)
-    vmem = pl.BlockSpec(memory_space=pltpu.VMEM)
-    sems = 3 * Gatherer.SEMS + 3
-    full = (4, 2, 4, 2, 16, ATTN_TOTAL)
-    return pl.pallas_call(
-        open_kernel,
-        out_shape=(
-            jax.ShapeDtypeStruct((HEADS, 256, WIDE), BF),
-            jax.ShapeDtypeStruct((256, D), BF),
-            jax.ShapeDtypeStruct((256, D), BF),
-            jax.ShapeDtypeStruct((4, 2, 4, 2, 16, 256), BF),
-            jax.ShapeDtypeStruct((TAIL, 256), BF),
-            jax.ShapeDtypeStruct((TAIL, QKV), BF),
-            jax.ShapeDtypeStruct((TAIL, D), BF),
-            jax.ShapeDtypeStruct((8, D), F32),
-            jax.ShapeDtypeStruct(full, BF),
-        ),
-        in_specs=[any_] + [vmem] * 10,
-        out_specs=(vmem,) * 8 + (any_,),
-        scratch_shapes=[
-            pltpu.VMEM(full, BF),
-            pltpu.VMEM((256, D), BF),
-            pltpu.VMEM((256, QKV), F32),
-            pltpu.VMEM((ATTN_CHUNK // LANES, LEAD, LANES), F32),
-            pltpu.VMEM((TAIL, 8 * ATTN_CHUNK), BF),
-            pltpu.VMEM((8, D), F32),
-            pltpu.SemaphoreType.DMA((sems,)),
-            pltpu.SemaphoreType.DMA((sems,)),
-            pltpu.SemaphoreType.DMA((1,)),
-        ],
-        compiler_params=mesh_params(tag),
-        name="open_layer",
-    )(slab, tokens, cotangent, *lines)
-
-
-def column_ids(row_ids):
-    size = row_ids.shape[1]
-    return jnp.transpose(jnp.broadcast_to(row_ids, (LANES, size)))
-
-
-def fetch_ids(picture, found, sem):
-    start = pl.multiple_of(lax.div(lax.axis_index("fsdp"), 8) * ROW, ROW)
-    return pltpu.make_async_copy(picture.at[:, pl.ds(start, ROW)], found, sem)
-
-
-def split_packed(packed, keys, queries):
-    lane = iota((ROW, LANES), 1)
-    zero = jnp.zeros((ROW, LANES), BF)
-    keys[...] = jnp.where(lane < HEAD_DIM, packed[:, :LANES], zero)
-    queries[...] = jnp.concatenate(
-        [packed[:, HEAD_DIM : 2 * HEAD_DIM], jnp.zeros((ROW, LANES - HEAD_DIM), BF)], axis=1
-    )
-
-
-def swap_only(swapper):
-    return [swapper.device(swapper.member(k)) for k in range(1, 16) if k not in (1, 4, 8, 12)]
-
-
-def attend_kernel(
+    vec_parts,
     heads,
-    slab,
-    picture,
-    packed_ref,
-    keep_ref,
-    o_all,
-    full,
     o_own,
     keys,
     queries,
@@ -1084,31 +982,98 @@
     local,
 ):
     place, core = here()
-    red = Gatherer(FIRST_WIDTHS, place, core, slab, full, send, recv, 0)
+    red = Gatherer(ATTN_WIDTHS, place, core, slab, full, send, recv, 0)
     base = 3 * Gatherer.SEMS + 3
-    swap_in = Swapper(place, core, heads, packed_ref, send, recv, base)
-    outs = [Swapper(place, core, o_own, o_all, send, recv, base + 16 + 16 * m) for m in range(2)]
-    greet(line_peers(place, core) + swap_only(swap_in))
+    first = Gatherer(FIRST_WIDTHS, place, core, first_slab, first_out, send, recv, base)
+    base = 2 * base
+    ins = [Swapper(place, core, heads, packed_ref, send, recv, base + 16 * m) for m in range(2)]
+    base = base + 32
+    outs = [Swapper(place, core, o_own, o_all, send, recv, base + 16 * m) for m in range(2)]
+    greet(line_peers(place, core) + swap_only(ins[0]))
     red.start()
-    swap_in.start()
     ids_in = fetch_ids(picture, found, local.at[0])
     ids_in.start()
+    for index, line in enumerate(lines):
+        vec_ref[index : index + 1, :] = line[...].reshape(1, D)
+    vec_parts[...] = exact_parts(vec_ref[...])
+
+    def mix(index, carry):
+        columns = lanes(index * LANES, LANES)
+        column = onehot(iota((D, LANES), 0) == origin(index * LANES + iota((D, LANES), 1)))
+        x_ref[:, columns] = dot(tokens_ref[...], column).astype(BF)
+        g_ref[:, columns] = dot(cotangent_ref[...], column).astype(BF)
+        parts = dot(vec_parts[...], column)
+        mixed_vec_ref[:, columns] = parts[0:8] + parts[8:16] + parts[16:24]
+        return carry
+
+    lax.fori_loop(0, 3, mix, 0)
+    red.second()
+    lax.fori_loop(3, 9, mix, 0)
+    unit, _ = normal(x_ref[...].astype(F32))
+    low[...] = (unit * mixed_vec_ref[0:1] + mixed_vec_ref[1:2]).astype(BF)
+    for steps in (1, 2, 3):
+        red.third(steps)
+    turned = jnp.transpose(low[...])
+    h_main_ref[...] = turned[:LEAD].reshape(4, 2, 4, 2, 16, 256)
+    h_tail_ref[...] = turned[LEAD:]
     ids_in.wait()
     for micro in range(2):
         row_ref[micro] = found[micro : micro + 1].astype(F32)
-    red.second()
-    for steps in (1, 2, 3):
-        red.third(steps)
-    swap_in.finish()
+    for steps in range(4):
+        red.fourth(steps)
+    first.start()
+    for steps in range(4):
+        red.fifth(steps)
+    first.second()
+    red.close()
+    leave = pltpu.make_async_copy(full, weight_out, local.at[1])
+    leave.start()
+
+    def packed_tile(tile):
+        start = ATTN_MAIN + tile * LANES
+        return full[:, :, :, :, :, start : start + LANES].reshape(LEAD, LANES)
+
+    spread_tail(packed_tile, ATTN_CHUNK, wide, tail)
+    tail_ref[...] = tail[:, :QKV]
+    out_tail_ref[...] = tail[:, QKV:ATTN_MAIN]
+    first.third(1)
+    first.third(2)
+
+    def columns(index, carry):
+        span = lanes(index * 384, 384)
+        weight = full[:, :, :, :, :, span].reshape(LEAD, 384)
+        flat[:, span] = dot(low[:, :LEAD], weight) + dot(low[:, LEAD:], tail[:, span])
+        return carry
+
+    lax.fori_loop(0, QKV // 384, columns, 0)
+    first.third(3)
+    for head in range(HEADS):
+        span = slice(head * HEAD_DIM, (head + 1) * HEAD_DIM)
+        bias = jnp.concatenate(
+            [jnp.zeros((1, HEAD_DIM), F32), vec_ref[6:7, span], vec_ref[7:8, span]], axis=1
+        )
+        block = flat[:, PACK * head : PACK * head + PACK] + bias
+        heads[head] = jnp.concatenate([block, jnp.zeros((256, WIDE - PACK), F32)], axis=1).astype(
+            BF
+        )
+    ins[0].start(0)
+    first.fourth(0)
+    first.fourth(1)
+    ins[1].start(1)
+    ins[0].finish(0)
 
     def block(step, carry):
         row = lax.div(step, 8)
         index = lax.rem(step, 8)
-        tokens = pl.ds(pl.multiple_of(row * 128, 128), 128)
+        rows_of = pl.ds(pl.multiple_of(row * 128, 128), 128)
+
+        @pl.when(step == 8)
+        def _():
+            ins[1].finish(1)
 
         @pl.when(index == 0)
         def _():
-            packed = packed_ref[:, tokens, :].reshape(ROW, WIDE)
+            packed = packed_ref[:, rows_of, :].reshape(ROW, WIDE)
             split_packed(packed, keys, queries)
             lane = iota((ROW, LANES), 1)
             values[...] = jnp.where(
@@ -1116,77 +1081,111 @@
             )
 
         rows = pl.ds(pl.multiple_of(index * 256, 256), 256)
-        query = queries[rows, :]
-        mine = column_ids(row_ref[row, :, lanes(index * 256, 256)])
-        mine = jnp.concatenate([mine] * (KEYS // LANES), axis=1)
-        top = jnp.full((256, LANES), NEG, F32)
-        for part in range(ROW // KEYS):
-            span = slice(part * KEYS, (part + 1) * KEYS)
-            score = dot_nt(query, keys[span, :])
-            score = jnp.where(mine == row_ref[row, :, span], score, NEG)
-            scores[:, span] = score
-            for lane_block in range(KEYS // LANES):
-                top = jnp.maximum(top, score[:, lane_block * LANES : (lane_block + 1) * LANES])
-        top = jnp.max(top, axis=1, keepdims=True)
-        total = jnp.zeros((256, LANES), F32)
-        for part in range(ROW // KEYS):
-            span = slice(part * KEYS, (part + 1) * KEYS)
-            expo = jnp.exp2((scores[:, span] - top) * (SCALE * LOG2E))
-            total = total + dot(expo.astype(BF), values[span, :])
-        mass = total[:, LANES - 1 :]
-        total = total / mass
-        o_own[pl.ds(index * 2, 2), tokens, :] = total.astype(BF).reshape(2, 128, LANES)
-        lane = iota((256, LANES), 1)
-        logsum = top * (SCALE * LOG2E) + jnp.log2(mass)
-        keep_ref[row, rows, :] = jnp.where(lane == 0, logsum, total)
-
-        @pl.when(lax.rem(step, 4) == 0)
+
+        def scan(count):
+            start = jnp.where(index < 4, 0, ROW - 256 * count)
+            query = queries[rows, :]
+            mine = column_ids(row_ref[row, :, lanes(index * 256, 256)])
+            mine = jnp.concatenate([mine, mine], axis=1)
+            top = jnp.full((256, LANES), NEG, F32)
+            for part in range(count):
+                span = lanes(start + part * 256, 256)
+                score = dot_nt(query, keys[span, :])
+                score = jnp.where(mine == row_ref[row, :, span], score, NEG)
+                scores[:, part * 256 : part * 256 + 256] = score
+                top = jnp.maximum(top, jnp.maximum(score[:, :LANES], score[:, LANES:]))
+            top = jnp.max(top, axis=1, keepdims=True)
+            total = jnp.zeros((256, LANES), F32)
+            for part in range(count):
+                span = lanes(start + part * 256, 256)
+                expo = jnp.exp2(
+                    (scores[:, part * 256 : part * 256 + 256] - top) * (SCALE * LOG2E)
+                )
+                total = total + dot(expo.astype(BF), values[span, :])
+            mass = total[:, LANES - 1 :]
+            total = total / mass
+            o_own[pl.ds(index * 2, 2), rows_of, :] = total.astype(BF).reshape(2, 128, LANES)
+            lane = iota((256, LANES), 1)
+            logsum = top * (SCALE * LOG2E) + jnp.log2(mass)
+            keep_ref[row, rows, :] = jnp.where(lane == 0, logsum, total)
+
+        for count in (5, 6, 7, 8):
+            pl.when((index == count - 5) | (index == 12 - count))(functools.partial(scan, count))
+
+        @pl.when(step == 2)
         def _():
-            red.fourth(lax.div(step, 4))
+            first.fourth(2)
+
+        @pl.when(step == 4)
+        def _():
+            first.fourth(3)
+
+        @pl.when((step >= 6) & (lax.rem(step, 2) == 0) & (step < 14))
+        def _():
+            first.fifth(lax.div(step - 6, 2))
 
         for micro in range(2):
             pl.when(step == 8 * micro + 7)(functools.partial(outs[micro].start, micro))
         return carry
 
     lax.fori_loop(0, 16, block, 0)
-    for steps in range(4):
-        red.fifth(steps)
-    red.close()
+    first.close()
+    leave.wait()
+    red.drain()
+    first.drain()
     for micro in range(2):
+        ins[micro].drain(micro)
         outs[micro].finish(micro)
-    red.drain()
-    swap_in.drain()
     for micro in range(2):
         outs[micro].drain(micro)
 
 
-def attend_gather(heads, slab, picture, tag):
+def front(slab, first_slab, tokens, cotangent, lines, picture, tag):
     any_ = pl.BlockSpec(memory_space=pl.ANY)
     vmem = pl.BlockSpec(memory_space=pltpu.VMEM)
-    sems = 3 * Gatherer.SEMS + 3 + 48
+    sems = 2 * (3 * Gatherer.SEMS + 3) + 64
+    full = (4, 2, 4, 2, 16, ATTN_TOTAL)
     return pl.pallas_call(
-        attend_kernel,
+        front_kernel,
         out_shape=(
+            jax.ShapeDtypeStruct((256, D), BF),
+            jax.ShapeDtypeStruct((256, D), BF),
+            jax.ShapeDtypeStruct((4, 2, 4, 2, 16, 256), BF),
+            jax.ShapeDtypeStruct((TAIL, 256), BF),
+            jax.ShapeDtypeStruct((TAIL, QKV), BF),
+            jax.ShapeDtypeStruct((TAIL, D), BF),
+            jax.ShapeDtypeStruct((8, D), F32),
             jax.ShapeDtypeStruct((16, 256, WIDE), BF),
             jax.ShapeDtypeStruct((2, ROW, LANES), F32),
             jax.ShapeDtypeStruct((16, 256, LANES), BF),
+            jax.ShapeDtypeStruct(full, BF),
             jax.ShapeDtypeStruct((4, 2, 4, 2, 16, FIRST_TOTAL), BF),
         ),
-        in_specs=[any_] * 3,
-        out_specs=(vmem, vmem, any_, any_),
-        scratch_shapes=[pltpu.VMEM((16, 256, LANES), BF)]
-        + [pltpu.VMEM((ROW, LANES), BF)] * 3
-        + [
+        in_specs=[any_] * 3 + [vmem] * 10,
+        out_specs=(vmem,) * 9 + (any_,) * 3,
+        scratch_shapes=[
+            pltpu.VMEM(full, BF),
+            pltpu.VMEM((256, D), BF),
+            pltpu.VMEM((256, QKV), F32),
+            pltpu.VMEM((ATTN_CHUNK // LANES, LEAD, LANES), F32),
+            pltpu.VMEM((TAIL, 8 * ATTN_CHUNK), BF),
+            pltpu.VMEM((8, D), F32),
+            pltpu.VMEM((24, D), BF),
+            pltpu.VMEM((16, 256, WIDE), BF),
+            pltpu.VMEM((16, 256, LANES), BF),
+            pltpu.VMEM((ROW, LANES), BF),
+            pltpu.VMEM((ROW, LANES), BF),
+            pltpu.VMEM((ROW, LANES), BF),
             pltpu.VMEM((256, ROW), F32),
             pltpu.VMEM((2, ROW), jnp.int32),
             pltpu.VMEM((2, 1, ROW), F32),
             pltpu.SemaphoreType.DMA((sems,)),
             pltpu.SemaphoreType.DMA((sems,)),
-            pltpu.SemaphoreType.DMA((1,)),
+            pltpu.SemaphoreType.DMA((2,)),
         ],
         compiler_params=mesh_params(tag),
-        name="attend_gather",
-    )(heads, slab, picture)
+        name="front",
+    )(slab, first_slab, picture, tokens, cotangent, *lines)
 
 
 def middle_kernel(
@@ -1199,6 +1198,8 @@
     out_b_ref,
     vec_ref,
     bias_ref,
+    place_ref,
+    pick_ref,
     mixed_ref,
     do_ref,
     dmid_ref,
@@ -1238,13 +1239,10 @@
     red.start()
     bias[...] = jnp.zeros_like(bias)
     bias[:, :FF] = bias_ref[...].reshape(1, FF)
-    mid[...] = jnp.zeros_like(mid)
-
-    def gather_head(head, carry):
-        mid[...] += dot(o_ref[head], head_place(head))
-        return carry
-
-    lax.fori_loop(0, HEADS, gather_head, 0)
+    for group in range(4):
+        block = jnp.concatenate([o_ref[4 * group + head] for head in range(4)], axis=1)
+        value = dot(block, place_ref[512 * group : 512 * group + 512, :])
+        mid[...] = value if group == 0 else mid[...] + value
     o_perm[...] = mid[...].astype(BF)
     red.second()
     out_in.wait()
@@ -1350,11 +1348,10 @@
     result[LEAD:] = dot(out_b_ref[...], low_t)
     o_perm[...] = jnp.transpose(result[...].astype(BF))
 
-    def split_head(head, carry):
-        do_ref[head] = dot(o_perm[...], head_pick(head)).astype(BF)
-        return carry
-
-    lax.fori_loop(0, HEADS, split_head, 0)
+    for group in range(4):
+        value = dot(o_perm[...], pick_ref[:, 512 * group : 512 * group + 512]).astype(BF)
+        for head in range(4):
+            do_ref[4 * group + head] = value[:, LANES * head : LANES * (head + 1)]
 
 
 def middle(attn, first, slab, o, x, g, out_tail, vec, bias, tag):
@@ -1362,6 +1359,7 @@
     vmem = pl.BlockSpec(memory_space=pltpu.VMEM)
     sems = 3 * Gatherer.SEMS + 3
     turned = [(4, 2, 4, 2, 16, 256), (TAIL, 256)] * 3
+    place = place_matrix().astype(BF)
     found = pl.pallas_call(
         middle_kernel,
         out_shape=tuple(
@@ -1377,7 +1375,7 @@
             ]
             + [jax.ShapeDtypeStruct(shape, BF) for shape in turned]
         ),
-        in_specs=[any_] * 3 + [vmem] * 6,
+        in_specs=[any_] * 3 + [vmem] * 8,
         out_specs=(vmem,) * 14,
         scratch_shapes=[
             pltpu.VMEM((LEAD, D), BF),
@@ -1397,7 +1395,7 @@
         ],
         compiler_params=mesh_params(tag),
         name="middle",
-    )(attn, first, slab, o, x, g, out_tail, vec, bias)
+    )(attn, first, slab, o, x, g, out_tail, vec, bias, place, place.T)
     return found[:8], found[12:14], found[8:10], found[10:12]
 
 
@@ -1525,47 +1523,33 @@
         (dy, dy_all, 0),
     ):
         twin.give(source, target, axis)
+    late_maker = Maker(
+        late,
+        [((h2_main_all, h2_tail_all), dpre_all), ((g_main_all, g_tail_all), active_all)],
+        extra.at[pl.ds(0, SECOND_CHUNK // LANES)],
+        SECOND_CHUNK,
+    )
+    maker = Maker(
+        red,
+        [((h_main_all, h_tail_all), flat_all), ((o_main_all, o_tail_all), dy_all)],
+        extra,
+        ATTN_CHUNK,
+    )
+    late_twin.ready()
+    late_maker.run()
     heads_in.wait()
     for head in range(HEADS):
         flat[:, PACK * head : PACK * head + PACK] = dheads_all[head, :, :PACK]
     twin.give(flat, flat_all, 0)
-
-    def make_all(reducer, maker):
-        maker.pack_tail()
-        for part in range(3):
-            maker.make(part, 2)
-        reducer.far_out()
-
-        def others(index, carry):
-            ahead = cycle(index, 3)
-            for part in range(3):
-                maker.make(part, ahead)
-            return carry
-
-        lax.fori_loop(0, 3, others, 0)
-
-    late_twin.ready()
-    make_all(
-        late,
-        Maker(
-            late,
-            [((h2_main_all, h2_tail_all), dpre_all), ((g_main_all, g_tail_all), active_all)],
-            extra.at[pl.ds(0, SECOND_CHUNK // LANES)],
-            SECOND_CHUNK,
-        ),
-    )
-    twin.ready()
-    make_all(
-        red,
-        Maker(
-            red,
-            [((h_main_all, h_tail_all), flat_all), ((o_main_all, o_tail_all), dy_all)],
-            extra,
-            ATTN_CHUNK,
-        ),
-    )
     for spot in range(4):
         late.pass_on(spot)
+    twin.ready()
+    maker.run()
+    for over in (2, 1, 3):
+        late.gather_side(over, False)
+    for spot in range(4):
+        red.pass_on(spot)
+    late.gather_side(0, True)
     dh[...] = jnp.zeros_like(dh)
     vectors[...] = jnp.zeros((VEC_ROWS, D), F32)
     vectors[2:6] = gvec_ref[:4]
@@ -1588,29 +1572,24 @@
             return carry
 
         lax.fori_loop(0, 3, columns, 0)
-    for spot in range(4):
-        red.pass_on(spot)
+    late.line_up()
     unit, rate = normal(x_ref[...].astype(F32))
     grad = jnp.transpose(dh[...])
     vectors[0:1] = column_total(grad * unit)
     vectors[1:2] = column_total(grad)
     every.start(0, vectors[...])
+    for over in (2, 1, 3):
+        red.gather_side(over, False)
+    every.start(1, every.finish(0))
     total = dmid_ref[...] + normal_back(unit, rate, vec_ref[0:1], grad)
     tokens_ref[...] = total.astype(BF)
-    for over in (2, 1, 3):
-        late.gather_side(over, False)
-    every.start(1, every.finish(0))
-    late.gather_side(0, True)
-    for over in (2, 1, 3):
-        red.gather_side(over, False)
+    red.gather_side(0, True)
+    late.share()
     every.start(2, every.finish(1))
-    red.gather_side(0, True)
-    late.line_up()
+    red.line_up()
     every.start(3, every.finish(2))
-    red.line_up()
-    late.share()
+    red.share()
     total_ref[...] = every.finish(3)
-    red.share()
     late.close()
     red.close()
     twin.drain()
@@ -1668,6 +1647,7 @@
     second_ref,
     mixed_in,
     tokens_in,
+    unmix_ref,
     mixed_ref,
     tokens_ref,
     query_ref,
@@ -1689,6 +1669,7 @@
     first,
     second,
     vec,
+    stack,
 ):
     def unpack(share, full, main, chunk):
         full[0:16, :] = share[:, :main].astype(F32)
@@ -1711,23 +1692,21 @@
         for index, ref in enumerate((key_ref, query_ref, value_ref)):
             start = head * PACK + index * HEAD_DIM
             ref[:, span] = attn[:18, start : start + HEAD_DIM]
-    low = attn[:, QKV:ATTN_MAIN].astype(BF)
-
-    def restore(index, carry):
-        columns = lanes(index * LANES, LANES)
-        matrix = unmix(index)
-        out_ref[:, columns] = dot(low, matrix)[:18]
-        mixed_ref[:, columns] = dot(mixed_in[...], matrix).astype(BF)
-        tokens_ref[:, columns] = dot(tokens_in[...], matrix).astype(BF)
-        vec[0:8, columns] = jnp.dot(
-            totals_ref[0:8, :],
-            matrix.astype(F32),
-            precision=lax.Precision.HIGHEST,
-            preferred_element_type=F32,
-        )
-        return carry
-
-    lax.fori_loop(0, 9, restore, 0)
+    stack[0:256] = mixed_in[...]
+    stack[256:512] = tokens_in[...]
+    stack[512:544] = jnp.concatenate(
+        [attn[:, QKV:ATTN_MAIN].astype(BF), jnp.zeros((8, D), BF)], axis=0
+    )
+    stack[544:576] = jnp.concatenate(
+        [exact_parts(totals_ref[0:8, :]), jnp.zeros((8, D), BF)], axis=0
+    )
+    for part in range(3):
+        columns = slice(384 * part, 384 * part + 384)
+        value = dot(stack[...], unmix_ref[:, columns])
+        mixed_ref[:, columns] = value[0:256].astype(BF)
+        tokens_ref[:, columns] = value[256:512].astype(BF)
+        out_ref[:, columns] = value[512:530]
+        vec[0:8, columns] = value[544:552] + value[552:560] + value[560:568]
     lines = (gain1_ref, bias1_ref, gain2_ref, bias2_ref, bias_out_ref, bias_down_ref)
     for index, ref in enumerate(lines):
         ref[...] = vec[index : index + 1, :D].reshape(D)
@@ -1774,10 +1753,11 @@
             pltpu.VMEM((24, 2 * FIRST), F32),
             pltpu.VMEM((24, 2 * SECOND), F32),
             pltpu.VMEM((16, 4 * D), F32),
+            pltpu.VMEM((576, D), BF),
         ],
         compiler_params=params(),
         name="close_layer",
-    )(totals, attn, first, second, mixed, tokens)
+    )(totals, attn, first, second, mixed, tokens, mix_matrix().T.astype(BF))
 
 
 def pack_slab(weight, chunk, total):
@@ -1834,11 +1814,16 @@
         jnp.concatenate([up[:, FIRST:], down[:, FIRST:]], axis=1), SECOND_CHUNK, SECOND_TOTAL
     )
     lines = (ln1_gain, ln1_bias, ln2_gain, ln2_bias, b_out, b_fc2, b_query, b_value)
-    heads, x, g, h_main, h_tail, attn_tail, out_tail, vec, attn = open_layer(
-        attn_slab, tokens.reshape(256, D), cotangent.reshape(256, D), lines, 0
+    x, g, h_main, h_tail, attn_tail, out_tail, vec, packed, keep, o, attn, first = front(
+        attn_slab,
+        first_slab,
+        tokens.reshape(256, D),
+        cotangent.reshape(256, D),
+        lines,
+        picture,
+        0,
     )
     attn = attn.reshape(LEAD, ATTN_TOTAL)
-    packed, keep, o, first = attend_gather(heads, first_slab, picture, 1)
     (mixed, go, dmid, dy, gvec2, gbias1, dpre, active), o_turned, h_turned, g_turned = middle(
         attn, first, second_slab, o, x, g, out_tail, vec, b_fc1, 2
     )

time: 340 us -> 316 us (0.929)
  Pallas kernels: 329 us -> 306 us
    pallas_call x2 -> x1, Pallas kernels: 118 us -> 109 us  [front(): pl.pallas_call(front_kernel, out_shape=(jax.ShapeDtypeStruct((256, D), BF...]
    pallas_call x1, Pallas kernels: 52.2 us -> 46 us  [middle(): pl.pallas_call(middle_kernel, out_shape=tuple([jax.ShapeDtypeStruct((256,...]
    pallas_call x1, Pallas kernels: 11.2 us -> 6.08 us  [close_layer(): pl.pallas_call(close_kernel, out_shape=(jax.ShapeDtypeStruct((256, D), BF...]
    pallas_call x1, Pallas kernels: 69.5 us -> 64.5 us  [finish(): pl.pallas_call(finish_kernel, out_shape=(jax.ShapeDtypeStruct((256, D), B...]
where the time goes in v1:
time: 316 us; the launch traced here: 313 us
  Pallas kernels  306 us (97%)
    pallas_call x1, Pallas kernels, front(): pl.pallas_call(front_kernel, out_shape=(jax.ShapeDtypeStruct((256, D), BF...  109 us
    pallas_call x1, Pallas kernels, attend_back_reduce(): pl.pallas_call(back_kernel, out_shape=(jax.ShapeDtypeStruct((16, FIRST_TO...  80.3 us
    pallas_call x1, Pallas kernels, finish(): pl.pallas_call(finish_kernel, out_shape=(jax.ShapeDtypeStruct((256, D), B...  64.5 us
    pallas_call x1, Pallas kernels, middle(): pl.pallas_call(middle_kernel, out_shape=tuple([jax.ShapeDtypeStruct((256,...  46 us

profile of v1, /device:TPU:0, one launch (start us, length us, event | category | flops | bytes accessed | tf_op | source)
XLA Modules:
  0.0 312.8 jit_solution(17259586062010807146)
XLA Ops:
  0.7 0.0 copy-start
  0.7 0.8 copy-done
  1.5 0.0 copy-start.1
  1.5 0.0 copy-start.2
  1.5 0.5 fusion.5
  2.0 0.5 copy-done.1
  2.4 0.1 copy-done.2
  2.5 0.0 copy-start.3
  2.5 0.0 copy-start.4
  2.5 0.0 copy-start.5
  2.6 0.7 pad_maximum_fusion.3.slab
  3.4 0.7 pad_maximum_fusion.1.first_slab
  4.1 0.0 copy-done.3
  4.1 0.3 reshape.83
  4.3 0.0 copy-done.4
  4.4 0.3 reshape.82
  4.6 0.0 copy-done.5
  4.6 0.3 reshape.84
  4.9 0.6 pad_maximum_fusion
  5.5 0.4 reshape.73
  6.0 0.7 pad_maximum_fusion.2.slab
  6.7 109.0 %front.1 = (bf16[256,1152]{1,0:T(8,128)(2,1)}, bf16[256,1152]{1,0:T(8,128)(2,1)}, bf16[4,2,4,2,16,256]{5,4,3,2,1,0:T(8,128)(2,1)}, bf16[128,256]{1,0:T(8,128)(2,...) custom-call(bf16[16,5376]{1,0:T(8,128)(2,1)} %pad_maximum_fusion.2.s, ...), custom_call_target="tpu_custom_call" | custom-call | tf_op jit(solution)/shard_map/front/pallas_call | solution.py:1148
  115.7 46.0 %middle.1 = (bf16[256,1152]{1,0:T(8,128)(2,1)}, bf16[16,256,128]{2,1,0:T(8,128)(2,1)}, f32[256,1152]{1,0:T(8,128)}, bf16[256,1152]{1,0:T(8,128)(2,1)}, f32[8,115...) custom-call(bf16[1024,5376]{1,0:T(8,128)(2,1)} %bitcast.10, ...), custom_call_target="tpu_custom_call" | custom-call | tf_op jit(solution)/shard_map/middle/pallas_call | solution.py:1363
  161.6 80.3 %attend_back_reduce.1 = (bf16[16,6912]{1,0:T(8,128)(2,1)}, bf16[16,256,256]{2,1,0:T(8,128)(2,1)}) custom-call(bf16[16,256,128]{2,1,0:T(8,128)(2,1)} %get-tuple-element.73.go, bf16[256,4352]{1,0:T(8,128)(2,1)} %get-tuple-element.74.dpre, bf16[256,4352]{1,0:T(8,128)(2,1)} %get-tuple-element.75.active, ...), custom_call_target="tpu_custom_call" | custom-call | tf_op jit(solution)/shard_map/attend_back_reduce/pallas_call | solution.py:860
  242.0 64.5 %finish.1 = (bf16[256,1152]{1,0:T(8,128)(2,1)}, f32[16,1152]{1,0:T(8,128)}, bf16[16,5376]{1,0:T(8,128)(2,1)}, bf16[16,3072]{1,0:T(8,128)(2,1)}) custom-call(bf16[16,256,256]{2,1,0:T(8,128)(2,1)} %get-tuple-element.82.dheads, bf16[1024,5376]{1,0:T(8,128)(2,1)} %bitcast.11, bf16[256,1152]{1,0:T(8,128)(2,1)} %get-tuple-element.83.dy, ...), custom_call_target="tpu_custom_call" | custom-call | tf_op jit(solution)/shard_map/finish/pallas_call | solution.py:1605
  306.5 6.1 %close_layer.1 = (bf16[256,1152]{1,0:T(8,128)(2,1)}, bf16[256,1152]{1,0:T(8,128)(2,1)}, f32[18,1152]{1,0:T(8,128)}, f32[18,1152]{1,0:T(8,128)}, f32[18,1152]{1,0...) custom-call(f32[16,1152]{1,0:T(8,128)} %get-tuple-element.92.totals_, ...), custom_call_target="tpu_custom_call" | custom-call | tf_op jit(solution)/shard_map/close_layer/pallas_call | solution.py:1737
  (15 shorter events, 0.2 us)
Async XLA Ops:
  0.7 0.8 copy-start
  1.5 0.9 copy-start.1
  1.5 1.0 copy-start.2
  2.5 1.6 copy-start.3
  2.5 1.8 copy-start.4
  2.5 2.1 copy-start.5

commit v2 on v1

--- a/solution.py
+++ b/solution.py
@@ -482,11 +482,11 @@
         return [self.device(self.member(k)) for k in range(1, 16)]
 
     def view(self, ref, index, micro):
-        if micro is None:
-            return ref.at[index]
-        return ref.at[index, pl.ds(micro * 128, 128)]
-
-    def start(self, micro=None):
+        if len(ref.shape) == 3:
+            return ref.at[index, :, pl.ds(micro * 128, 128)]
+        return ref.at[:, pl.ds(pl.multiple_of(micro * ROW + index * 128, 128), 128)]
+
+    def start(self, micro):
         for k in SWAP_ORDER:
             target = self.member(k)
             remote(
@@ -502,7 +502,7 @@
             self.send.at[self.base],
         ).start()
 
-    def finish(self, micro=None):
+    def finish(self, micro):
         pltpu.make_async_copy(
             self.view(self.own, self.mine, micro),
             self.view(self.full, self.mine, micro),
@@ -518,7 +518,7 @@
                 self.device(self.mine),
             ).wait_recv()
 
-    def drain(self, micro=None):
+    def drain(self, micro):
         for k in range(1, 16):
             region = self.view(self.own, self.member(k), micro)
             remote(
@@ -550,6 +550,8 @@
 TAIL = 128
 PACK = 3 * HEAD_DIM
 WIDE = 256
+WIRE = 224
+HEAD_WIRE = 80
 VALUE_LANE = 16
 FF_PAD = 4352
 QKV = HEADS * PACK
@@ -652,10 +654,9 @@
 
 
 def place_matrix():
-    matrix = np.zeros((HEADS, LANES, D), np.float32)
-    mixed = mix_matrix().reshape(HEADS, HEAD_DIM, D)
-    matrix[:, VALUE_LANE : VALUE_LANE + HEAD_DIM] = mixed
-    return matrix.reshape(HEADS * LANES, D)
+    matrix = np.zeros((HEADS, HEAD_WIRE, D), np.float32)
+    matrix[:, :HEAD_DIM] = mix_matrix().reshape(HEADS, HEAD_DIM, D)
+    return matrix.reshape(HEADS * HEAD_WIRE, D)
 
 
 def mesh_params(tag, limit=62):
@@ -692,6 +693,21 @@
             remote(
                 other, other, self.send.at[index], self.recv.at[index], self.device
             ).wait_recv()
+
+    def pass_part(self, source, target, columns, number):
+        index = self.base + 2 * number
+        place = target.at[pl.ds(pl.multiple_of(self.core * 256, 256), 256), columns]
+        pltpu.make_async_copy(source, place, self.recv.at[index + 1]).start()
+        remote(source, place, self.send.at[index], self.recv.at[index], self.device).start()
+
+    def part_done(self, target, columns, number):
+        index = self.base + 2 * number
+        place = target.at[pl.ds(pl.multiple_of(self.core * 256, 256), 256), columns]
+        other = target.at[pl.ds(pl.multiple_of((1 - self.core) * 256, 256), 256), columns]
+        pltpu.make_async_copy(place, place, self.recv.at[index + 1]).wait()
+        copy = remote(other, other, self.send.at[index], self.recv.at[index], self.device)
+        copy.wait_recv()
+        copy.wait_send()
 
     def drain(self):
         for source, target, axis, index in self.items:
@@ -716,6 +732,8 @@
     dheads,
     go_all,
     grads,
+    wire,
+    backs,
     dpre_all,
     active_all,
     h_main_all,
@@ -736,20 +754,24 @@
     place, core = here()
     red = Reducer(FIRST_WIDTHS, place, core, buffers, share_ref, send, recv)
     base = 3 * Reducer.SEMS
-    swap_in = Swapper(place, core, go, go_all, send, recv, base)
-    outs = [Swapper(place, core, grads, dheads, send, recv, base + 16 + 16 * m) for m in range(2)]
-    twin = Twin(place, core, send, recv, base + 48)
-    greet(line_peers(place, core) + swap_only(swap_in))
-    swap_in.start()
-    for source, target, axis in (
-        (h_main, h_main_all, 5),
-        (h_tail, h_tail_all, 1),
-        (g_main, g_main_all, 5),
-        (g_tail, g_tail_all, 1),
-        (dpre.at[:, pl.ds(0, FIRST)], dpre_all, 0),
-        (active.at[:, pl.ds(0, FIRST)], active_all, 0),
+    ins = [Swapper(place, core, go, go_all, send, recv, base + 16 * m) for m in range(2)]
+    base = base + 32
+    outs = [Swapper(place, core, wire, dheads, send, recv, base + 16 * m) for m in range(2)]
+    greet(line_peers(place, core) + swap_only(ins[0]))
+    for micro in range(2):
+        ins[micro].start(micro)
+    loads = []
+    for source, target in (
+        (h_main, h_main_all),
+        (h_tail, h_tail_all),
+        (g_main, g_main_all),
+        (g_tail, g_tail_all),
+        (dpre.at[:, pl.ds(0, FIRST)], dpre_all),
+        (active.at[:, pl.ds(0, FIRST)], active_all),
     ):
-        twin.give(source, target, axis)
+        copy = pltpu.make_async_copy(source, target, local.at[1 + len(loads)])
+        copy.start()
+        loads.append(copy)
     maker = Maker(
         red,
         [((h_main_all, h_tail_all), dpre_all), ((g_main_all, g_tail_all), active_all)],
@@ -761,17 +783,33 @@
     ids_in.wait()
     for micro in range(2):
         row_ref[micro] = found[micro : micro + 1].astype(F32)
-    twin.ready()
+    for copy in loads:
+        copy.wait()
     maker.run()
-    swap_in.finish()
+    for spot in range(4):
+        red.pass_on(spot)
+    ins[0].finish(0)
 
     def block(step, carry):
         row = lax.div(step, BLOCKS)
         index = lax.rem(step, BLOCKS)
         tokens = pl.ds(pl.multiple_of(row * 128, 128), 128)
 
+        @pl.when(step == BLOCKS)
+        def _():
+            ins[1].finish(1)
+
         @pl.when(index == 0)
         def _():
+            back_row = jnp.concatenate(
+                [
+                    jnp.zeros((VALUE_LANE, ROW), BF),
+                    go_all[:, lanes(row * ROW, ROW)],
+                    jnp.zeros((LANES - VALUE_LANE - HEAD_WIRE, ROW), BF),
+                ],
+                axis=0,
+            )
+            backs[...] = jnp.transpose(back_row)
             packed = packed_ref[:, tokens, :].reshape(ROW, WIDE)
             split_packed(packed, keys, queries)
             for part in range(ROW // LANES):
@@ -781,12 +819,11 @@
             dvalues[...] = jnp.zeros_like(dvalues)
 
         rows = pl.ds(pl.multiple_of(index * QUERIES, QUERIES), QUERIES)
-        groups = pl.ds(index * (QUERIES // 128), QUERIES // 128)
 
         def scan(count):
             start = jnp.where(index < 2, 0, BLOCKS - count)
             query = queries[rows, :]
-            back = go_all[groups, tokens, :].reshape(QUERIES, LANES)
+            back = backs[rows, :]
             mine = row_ref[row, :, lanes(index * QUERIES, QUERIES)]
             kept = keep_ref[row, rows, :]
             inner = jnp.sum(back.astype(F32) * kept, axis=1, keepdims=True)
@@ -815,7 +852,7 @@
                 ],
                 axis=1,
             )
-            grads[groups, tokens, :] = moved_q.astype(BF).reshape(QUERIES // 128, 128, WIDE)
+            grads[rows, :] = moved_q.astype(BF)
 
         edge = (index == 0) | (index == BLOCKS - 1)
         pl.when(edge)(functools.partial(scan, 3))
@@ -825,15 +862,12 @@
         def _():
             wide = jnp.concatenate([dkeys[...] * SCALE, dvalues[...]], axis=1)
             lane = iota((ROW, WIDE), 1)
-            old = grads[:, tokens, :].reshape(ROW, WIDE)
+            old = grads[...]
             inside = (lane >= HEAD_DIM) & (lane < 2 * HEAD_DIM)
-            grads[:, tokens, :] = jnp.where(inside, old, wide.astype(BF)).reshape(16, 128, WIDE)
+            whole = jnp.where(inside, old, wide.astype(BF))
+            wire[:, lanes(row * ROW, ROW)] = jnp.transpose(whole)[:WIRE]
             for micro in range(2):
                 pl.when(row == micro)(functools.partial(outs[micro].start, micro))
-
-        @pl.when(step < 4)
-        def _():
-            red.pass_on(step)
 
         @pl.when(step >= 4)
         def _():
@@ -847,27 +881,29 @@
     red.close()
     for micro in range(2):
         outs[micro].finish(micro)
-    swap_in.drain()
+    for micro in range(2):
+        ins[micro].drain(micro)
     for micro in range(2):
         outs[micro].drain(micro)
-    twin.drain()
 
 
 def attend_back_reduce(go, dpre, active, turned, packed, keep, picture, tag):
     any_ = pl.BlockSpec(memory_space=pl.ANY)
     vmem = pl.BlockSpec(memory_space=pltpu.VMEM)
-    sems = 3 * Reducer.SEMS + 48 + 12
+    sems = 3 * Reducer.SEMS + 64
     return pl.pallas_call(
         back_kernel,
         out_shape=(
             jax.ShapeDtypeStruct((16, FIRST_TOTAL), BF),
-            jax.ShapeDtypeStruct((16, 256, WIDE), BF),
+            jax.ShapeDtypeStruct((16, WIRE, 256), BF),
         ),
         in_specs=[any_] * 8 + [vmem] * 2,
         out_specs=(vmem, any_),
         scratch_shapes=[
-            pltpu.VMEM((16, 256, LANES), BF),
-            pltpu.VMEM((16, 256, WIDE), BF),
+            pltpu.VMEM((HEAD_WIRE, 2 * ROW), BF),
+            pltpu.VMEM((ROW, WIDE), BF),
+            pltpu.VMEM((WIRE, 2 * ROW), BF),
+            pltpu.VMEM((ROW, LANES), BF),
             pltpu.VMEM((512, FIRST), BF),
             pltpu.VMEM((512, FIRST), BF),
             pltpu.VMEM((4, 2, 4, 2, 16, 512), BF),
@@ -887,7 +923,7 @@
         + [
             pltpu.SemaphoreType.DMA((sems,)),
             pltpu.SemaphoreType.DMA((sems,)),
-            pltpu.SemaphoreType.DMA((1,)),
+            pltpu.SemaphoreType.DMA((7,)),
         ],
         compiler_params=mesh_params(tag),
         name="attend_back_reduce",
@@ -952,8 +988,6 @@
     lines,
     x_ref,
     g_ref,
-    h_main_ref,
-    h_tail_ref,
     tail_ref,
     out_tail_ref,
     mixed_vec_ref,
@@ -962,6 +996,10 @@
     o_all,
     weight_out,
     first_out,
+    h_main_all,
+    h_tail_all,
+    h_main,
+    h_tail,
     full,
     low,
     flat,
@@ -970,6 +1008,7 @@
     vec_ref,
     vec_parts,
     heads,
+    wire,
     o_own,
     keys,
     queries,
@@ -986,11 +1025,13 @@
     base = 3 * Gatherer.SEMS + 3
     first = Gatherer(FIRST_WIDTHS, place, core, first_slab, first_out, send, recv, base)
     base = 2 * base
-    ins = [Swapper(place, core, heads, packed_ref, send, recv, base + 16 * m) for m in range(2)]
+    ins = [Swapper(place, core, heads, wire, send, recv, base + 16 * m) for m in range(2)]
     base = base + 32
     outs = [Swapper(place, core, o_own, o_all, send, recv, base + 16 * m) for m in range(2)]
+    twin = Twin(place, core, send, recv, base + 32)
     greet(line_peers(place, core) + swap_only(ins[0]))
     red.start()
+    first.start()
     ids_in = fetch_ids(picture, found, local.at[0])
     ids_in.start()
     for index, line in enumerate(lines):
@@ -1014,17 +1055,18 @@
     for steps in (1, 2, 3):
         red.third(steps)
     turned = jnp.transpose(low[...])
-    h_main_ref[...] = turned[:LEAD].reshape(4, 2, 4, 2, 16, 256)
-    h_tail_ref[...] = turned[LEAD:]
+    h_main[...] = turned[:LEAD].reshape(4, 2, 4, 2, 16, 256)
+    h_tail[...] = turned[LEAD:]
+    twin.give(h_main, h_main_all, 5)
+    twin.give(h_tail, h_tail_all, 1)
     ids_in.wait()
     for micro in range(2):
         row_ref[micro] = found[micro : micro + 1].astype(F32)
     for steps in range(4):
         red.fourth(steps)
-    first.start()
+    first.second()
     for steps in range(4):
         red.fifth(steps)
-    first.second()
     red.close()
     leave = pltpu.make_async_copy(full, weight_out, local.at[1])
     leave.start()
@@ -1033,11 +1075,11 @@
         start = ATTN_MAIN + tile * LANES
         return full[:, :, :, :, :, start : start + LANES].reshape(LEAD, LANES)
 
+    for steps in (1, 2, 3):
+        first.third(steps)
     spread_tail(packed_tile, ATTN_CHUNK, wide, tail)
     tail_ref[...] = tail[:, :QKV]
     out_tail_ref[...] = tail[:, QKV:ATTN_MAIN]
-    first.third(1)
-    first.third(2)
 
     def columns(index, carry):
         span = lanes(index * 384, 384)
@@ -1046,16 +1088,14 @@
         return carry
 
     lax.fori_loop(0, QKV // 384, columns, 0)
-    first.third(3)
     for head in range(HEADS):
         span = slice(head * HEAD_DIM, (head + 1) * HEAD_DIM)
         bias = jnp.concatenate(
             [jnp.zeros((1, HEAD_DIM), F32), vec_ref[6:7, span], vec_ref[7:8, span]], axis=1
         )
         block = flat[:, PACK * head : PACK * head + PACK] + bias
-        heads[head] = jnp.concatenate([block, jnp.zeros((256, WIDE - PACK), F32)], axis=1).astype(
-            BF
-        )
+        block = jnp.concatenate([block, jnp.zeros((256, WIDE - PACK), F32)], axis=1)
+        heads[head] = jnp.transpose(block.astype(BF))[:WIRE]
     ins[0].start(0)
     first.fourth(0)
     first.fourth(1)
@@ -1073,7 +1113,9 @@
 
         @pl.when(index == 0)
         def _():
-            packed = packed_ref[:, rows_of, :].reshape(ROW, WIDE)
+            packed = jnp.transpose(wire[:, lanes(row * ROW, ROW)])
+            packed = jnp.concatenate([packed, jnp.zeros((ROW, WIDE - WIRE), BF)], axis=1)
+            packed_ref[:, rows_of, :] = packed.reshape(16, 128, WIDE)
             split_packed(packed, keys, queries)
             lane = iota((ROW, LANES), 1)
             values[...] = jnp.where(
@@ -1104,7 +1146,8 @@
                 total = total + dot(expo.astype(BF), values[span, :])
             mass = total[:, LANES - 1 :]
             total = total / mass
-            o_own[pl.ds(index * 2, 2), rows_of, :] = total.astype(BF).reshape(2, 128, LANES)
+            turned_o = jnp.transpose(total)[VALUE_LANE : VALUE_LANE + HEAD_WIRE]
+            o_own[:, lanes(row * ROW + index * 256, 256)] = turned_o.astype(BF)
             lane = iota((256, LANES), 1)
             logsum = top * (SCALE * LOG2E) + jnp.log2(mass)
             keep_ref[row, rows, :] = jnp.where(lane == 0, logsum, total)
@@ -1138,32 +1181,36 @@
         outs[micro].finish(micro)
     for micro in range(2):
         outs[micro].drain(micro)
+    twin.ready()
+    twin.drain()
 
 
 def front(slab, first_slab, tokens, cotangent, lines, picture, tag):
     any_ = pl.BlockSpec(memory_space=pl.ANY)
     vmem = pl.BlockSpec(memory_space=pltpu.VMEM)
-    sems = 2 * (3 * Gatherer.SEMS + 3) + 64
+    sems = 2 * (3 * Gatherer.SEMS + 3) + 64 + 4
     full = (4, 2, 4, 2, 16, ATTN_TOTAL)
     return pl.pallas_call(
         front_kernel,
         out_shape=(
             jax.ShapeDtypeStruct((256, D), BF),
             jax.ShapeDtypeStruct((256, D), BF),
-            jax.ShapeDtypeStruct((4, 2, 4, 2, 16, 256), BF),
-            jax.ShapeDtypeStruct((TAIL, 256), BF),
             jax.ShapeDtypeStruct((TAIL, QKV), BF),
             jax.ShapeDtypeStruct((TAIL, D), BF),
             jax.ShapeDtypeStruct((8, D), F32),
             jax.ShapeDtypeStruct((16, 256, WIDE), BF),
             jax.ShapeDtypeStruct((2, ROW, LANES), F32),
-            jax.ShapeDtypeStruct((16, 256, LANES), BF),
+            jax.ShapeDtypeStruct((16, HEAD_WIRE, 256), BF),
             jax.ShapeDtypeStruct(full, BF),
             jax.ShapeDtypeStruct((4, 2, 4, 2, 16, FIRST_TOTAL), BF),
+            jax.ShapeDtypeStruct((4, 2, 4, 2, 16, 512), BF),
+            jax.ShapeDtypeStruct((TAIL, 512), BF),
         ),
         in_specs=[any_] * 3 + [vmem] * 10,
-        out_specs=(vmem,) * 9 + (any_,) * 3,
+        out_specs=(vmem,) * 7 + (any_,) * 5,
         scratch_shapes=[
+            pltpu.VMEM((4, 2, 4, 2, 16, 256), BF),
+            pltpu.VMEM((TAIL, 256), BF),
             pltpu.VMEM(full, BF),
             pltpu.VMEM((256, D), BF),
             pltpu.VMEM((256, QKV), F32),
@@ -1171,8 +1218,9 @@
             pltpu.VMEM((TAIL, 8 * ATTN_CHUNK), BF),
             pltpu.VMEM((8, D), F32),
             pltpu.VMEM((24, D), BF),
-            pltpu.VMEM((16, 256, WIDE), BF),
-            pltpu.VMEM((16, 256, LANES), BF),
+            pltpu.VMEM((16, WIRE, 256), BF),
+            pltpu.VMEM((WIRE, 2 * ROW), BF),
+            pltpu.VMEM((HEAD_WIRE, 2 * ROW), BF),
             pltpu.VMEM((ROW, LANES), BF),
             pltpu.VMEM((ROW, LANES), BF),
             pltpu.VMEM((ROW, LANES), BF),
@@ -1199,13 +1247,21 @@
     vec_ref,
     bias_ref,
     place_ref,
-    pick_ref,
     mixed_ref,
     do_ref,
     dmid_ref,
-    dy_ref,
     gvec_ref,
     gbias_ref,
+    dy_all,
+    dpre_all,
+    active_all,
+    h_main_all,
+    h_tail_all,
+    g_main_all,
+    g_tail_all,
+    o_main_all,
+    o_tail_all,
+    dy,
     dpre_ref,
     active_ref,
     h_main_ref,
@@ -1235,15 +1291,15 @@
     out_in.start()
     first_in = pltpu.make_async_copy(first, weights, local.at[1])
     first_in.start()
+    base = 3 * Gatherer.SEMS + 3
+    twin = Twin(place, core, send, recv, base)
+    chunks = Twin(place, core, send, recv, base + 14)
     greet(line_peers(place, core) + [device_at(place, 1 - core)])
     red.start()
     bias[...] = jnp.zeros_like(bias)
     bias[:, :FF] = bias_ref[...].reshape(1, FF)
-    for group in range(4):
-        block = jnp.concatenate([o_ref[4 * group + head] for head in range(4)], axis=1)
-        value = dot(block, place_ref[512 * group : 512 * group + 512, :])
-        mid[...] = value if group == 0 else mid[...] + value
-    o_perm[...] = mid[...].astype(BF)
+    blocks = jnp.transpose(o_ref[...].reshape(HEADS * HEAD_WIRE, 256))
+    o_perm[...] = dot(blocks, place_ref[...]).astype(BF)
     red.second()
     out_in.wait()
     for part in range(3):
@@ -1256,14 +1312,16 @@
     for steps in (1, 2, 3):
         red.third(steps)
 
-    def turn(value, main, rest):
+    def turn(value, main, rest, main_all, rest_all):
         turned = jnp.transpose(value)
         main[...] = turned[:LEAD].reshape(4, 2, 4, 2, 16, 256)
         rest[...] = turned[LEAD:]
-
-    turn(o_perm[...], o_main_ref, o_tail_ref)
-    turn(h2[...], h_main_ref, h_tail_ref)
-    turn(g_ref[...], g_main_ref, g_tail_ref)
+        twin.give(main, main_all, 5)
+        twin.give(rest, rest_all, 1)
+
+    turn(o_perm[...], o_main_ref, o_tail_ref, o_main_all, o_tail_all)
+    turn(h2[...], h_main_ref, h_tail_ref, h_main_all, h_tail_all)
+    turn(g_ref[...], g_main_ref, g_tail_ref, g_main_all, g_tail_all)
     result[...] = jnp.zeros_like(result)
     dh2[...] = jnp.zeros_like(dh2)
     first_in.wait()
@@ -1279,7 +1337,11 @@
     red.fourth(0)
     red.fourth(1)
 
-    def chunk(ref, span, width, index, size):
+    def deliver(number, place_all):
+        for item, (source, target) in enumerate(((dpre_ref, dpre_all), (active_ref, active_all))):
+            chunks.pass_part(source.at[:, place_all], target, place_all, 2 * number + item)
+
+    def chunk(ref, span, width, index, size, number):
         up_place = lanes(index * size, size)
         down_place = lanes(width + index * size, size)
         place_all = lanes(span + index * size, size)
@@ -1304,9 +1366,10 @@
         dh2[:LEAD] += dot(up, dpre_t)
         dh2[LEAD:] += dot(up_tail, dpre_t)
         gbias_ref[:, place_all] = column_total(dpre.astype(F32))
+        deliver(number, place_all)
 
     def early(index, carry):
-        chunk(weights, 0, FIRST, index, FIRST_STEP)
+        chunk(weights, 0, FIRST, index, FIRST_STEP, index)
 
         @pl.when(index == 0)
         def _():
@@ -1325,7 +1388,7 @@
     spread_tail(tile_of(full, 2 * SECOND), SECOND_CHUNK, wide, tail)
 
     def late(index, carry):
-        chunk(full, FIRST, SECOND, index, SECOND_STEP)
+        chunk(full, FIRST, SECOND, index, SECOND_STEP, index + FIRST // FIRST_STEP)
         return carry
 
     lax.fori_loop(0, SECOND // SECOND_STEP, late, 0)
@@ -1340,44 +1403,56 @@
     dmid = g_ref[...].astype(F32) + normal_back(unit, rate, gain, grad)
     dmid_ref[...] = dmid
     dlow = dmid.astype(BF)
-    dy_ref[...] = dlow
+    dy[...] = dlow
+    twin.give(dy, dy_all, 0)
     gvec_ref[2:3] = column_total(dlow.astype(F32))
     mixed_ref[...] = (mid[...] + jnp.transpose(result[...]) + vec_ref[5:6]).astype(BF)
     low_t = jnp.transpose(dlow)
     result[:LEAD] = dot(out_a[...], low_t)
     result[LEAD:] = dot(out_b_ref[...], low_t)
-    o_perm[...] = jnp.transpose(result[...].astype(BF))
-
-    for group in range(4):
-        value = dot(o_perm[...], pick_ref[:, 512 * group : 512 * group + 512]).astype(BF)
-        for head in range(4):
-            do_ref[4 * group + head] = value[:, LANES * head : LANES * (head + 1)]
+    value = dot(place_ref[...], result[...].astype(BF)).astype(BF)
+    do_ref[...] = value.reshape(HEADS, HEAD_WIRE, 256)
+    twin.ready()
+    twin.drain()
+    number = 0
+    for start, stop, size in ((0, FIRST, FIRST_STEP), (FIRST, FF_PAD, SECOND_STEP)):
+        for spot in range(start, stop, size):
+            for item, target in enumerate((dpre_all, active_all)):
+                chunks.part_done(target, pl.ds(spot, size), 2 * number + item)
+            number += 1
 
 
 def middle(attn, first, slab, o, x, g, out_tail, vec, bias, tag):
     any_ = pl.BlockSpec(memory_space=pl.ANY)
     vmem = pl.BlockSpec(memory_space=pltpu.VMEM)
-    sems = 3 * Gatherer.SEMS + 3
+    sems = 3 * Gatherer.SEMS + 3 + 14 + 24
     turned = [(4, 2, 4, 2, 16, 256), (TAIL, 256)] * 3
+    both = [(4, 2, 4, 2, 16, 512), (TAIL, 512)] * 3
     place = place_matrix().astype(BF)
     found = pl.pallas_call(
         middle_kernel,
         out_shape=tuple(
             [
                 jax.ShapeDtypeStruct((256, D), BF),
-                jax.ShapeDtypeStruct((HEADS, 256, LANES), BF),
+                jax.ShapeDtypeStruct((HEADS, HEAD_WIRE, 256), BF),
                 jax.ShapeDtypeStruct((256, D), F32),
-                jax.ShapeDtypeStruct((256, D), BF),
                 jax.ShapeDtypeStruct((8, D), F32),
                 jax.ShapeDtypeStruct((1, FF_PAD), F32),
-                jax.ShapeDtypeStruct((256, FF_PAD), BF),
-                jax.ShapeDtypeStruct((256, FF_PAD), BF),
+                jax.ShapeDtypeStruct((512, D), BF),
+                jax.ShapeDtypeStruct((512, FF_PAD), BF),
+                jax.ShapeDtypeStruct((512, FF_PAD), BF),
             ]
-            + [jax.ShapeDtypeStruct(shape, BF) for shape in turned]
+            + [jax.ShapeDtypeStruct(shape, BF) for shape in both]
         ),
-        in_specs=[any_] * 3 + [vmem] * 8,
-        out_specs=(vmem,) * 14,
+        in_specs=[any_] * 3 + [vmem] * 7,
+        out_specs=(vmem,) * 5 + (any_,) * 9,
         scratch_shapes=[
+            pltpu.VMEM((256, D), BF),
+            pltpu.VMEM((256, FF_PAD), BF),
+            pltpu.VMEM((256, FF_PAD), BF),
+        ]
+        + [pltpu.VMEM(shape, BF) for shape in turned]
+        + [
             pltpu.VMEM((LEAD, D), BF),
             pltpu.VMEM((4, 2, 4, 2, 16, FIRST_TOTAL), BF),
             pltpu.VMEM((4, 2, 4, 2, 16, SECOND_TOTAL), BF),
@@ -1395,7 +1470,7 @@
         ],
         compiler_params=mesh_params(tag),
         name="middle",
-    )(attn, first, slab, o, x, g, out_tail, vec, bias, place, place.T)
+    )(attn, first, slab, o, x, g, out_tail, vec, bias, place)
     return found[:8], found[12:14], found[8:10], found[10:12]
 
 
@@ -1499,30 +1574,34 @@
     late = Reducer(SECOND_WIDTHS, place, core, buffers[18:], second_ref, send, recv, base)
     base = 2 * base
     twin = Twin(place, core, send, recv, base)
-    late_twin = Twin(place, core, send, recv, base + 12)
-    every = Everyone(place, core, slots, send, recv, base + 24)
+    every = Everyone(place, core, slots, send, recv, base + 2)
     heads_in = pltpu.make_async_copy(dheads, dheads_all, local.at[0])
     heads_in.start()
     weight_in = pltpu.make_async_copy(weight.at[:, pl.ds(0, QKV)], weight_all, local.at[1])
     weight_in.start()
     greet(line_peers(place, core) + [device_at(place, 1 - core)])
-    for source, target, axis in (
-        (h2_main, h2_main_all, 5),
-        (h2_tail, h2_tail_all, 1),
-        (dpre.at[:, pl.ds(FIRST, SECOND)], dpre_all, 0),
-        (g_main, g_main_all, 5),
-        (g_tail, g_tail_all, 1),
-        (active.at[:, pl.ds(FIRST, SECOND)], active_all, 0),
+    loads = []
+    for source, target in (
+        (h_main, h_main_all),
+        (h_tail, h_tail_all),
+        (o_main, o_main_all),
+        (o_tail, o_tail_all),
+        (dy, dy_all),
+        (h2_main, h2_main_all),
+        (h2_tail, h2_tail_all),
+        (g_main, g_main_all),
+        (g_tail, g_tail_all),
+        (dpre.at[:, pl.ds(FIRST, SECOND)], dpre_all),
+        (active.at[:, pl.ds(FIRST, SECOND)], active_all),
     ):
-        late_twin.give(source, target, axis)
-    for source, target, axis in (
-        (h_main, h_main_all, 5),
-        (h_tail, h_tail_all, 1),
-        (o_main, o_main_all, 5),
-        (o_tail, o_tail_all, 1),
-        (dy, dy_all, 0),
-    ):
-        twin.give(source, target, axis)
+        copy = pltpu.make_async_copy(source, target, local.at[2 + len(loads)])
+        copy.start()
+        loads.append(copy)
+    heads_in.wait()
+    for head in range(HEADS):
+        flat[:, PACK * head : PACK * head + PACK] = jnp.transpose(dheads_all[head])[:, :PACK]
+    twin.give(flat, flat_all, 0)
+
     late_maker = Maker(
         late,
         [((h2_main_all, h2_tail_all), dpre_all), ((g_main_all, g_tail_all), active_all)],
@@ -1535,21 +1614,11 @@
         extra,
         ATTN_CHUNK,
     )
-    late_twin.ready()
+    for copy in loads:
+        copy.wait()
     late_maker.run()
-    heads_in.wait()
-    for head in range(HEADS):
-        flat[:, PACK * head : PACK * head + PACK] = dheads_all[head, :, :PACK]
-    twin.give(flat, flat_all, 0)
-    for spot in range(4):
-        late.pass_on(spot)
     twin.ready()
     maker.run()
-    for over in (2, 1, 3):
-        late.gather_side(over, False)
-    for spot in range(4):
-        red.pass_on(spot)
-    late.gather_side(0, True)
     dh[...] = jnp.zeros_like(dh)
     vectors[...] = jnp.zeros((VEC_ROWS, D), F32)
     vectors[2:6] = gvec_ref[:4]
@@ -1572,35 +1641,41 @@
             return carry
 
         lax.fori_loop(0, 3, columns, 0)
-    late.line_up()
+    for spot in range(4):
+        late.pass_on(spot)
     unit, rate = normal(x_ref[...].astype(F32))
     grad = jnp.transpose(dh[...])
     vectors[0:1] = column_total(grad * unit)
     vectors[1:2] = column_total(grad)
     every.start(0, vectors[...])
+    for spot in range(4):
+        red.pass_on(spot)
+    total = dmid_ref[...] + normal_back(unit, rate, vec_ref[0:1], grad)
+    tokens_ref[...] = total.astype(BF)
+    every.start(1, every.finish(0))
+    for over in (2, 1, 3):
+        late.gather_side(over, False)
+    late.gather_side(0, True)
+    every.start(2, every.finish(1))
     for over in (2, 1, 3):
         red.gather_side(over, False)
-    every.start(1, every.finish(0))
-    total = dmid_ref[...] + normal_back(unit, rate, vec_ref[0:1], grad)
-    tokens_ref[...] = total.astype(BF)
     red.gather_side(0, True)
+    every.start(3, every.finish(2))
+    late.line_up()
+    red.line_up()
     late.share()
-    every.start(2, every.finish(1))
-    red.line_up()
-    every.start(3, every.finish(2))
+    total_ref[...] = every.finish(3)
     red.share()
-    total_ref[...] = every.finish(3)
     late.close()
     red.close()
     twin.drain()
-    late_twin.drain()
     every.drain()
 
 
 def finish(dheads, weight, dy, dpre, active, turned, tail, x, dmid, vec, gvec, gup, tag):
     any_ = pl.BlockSpec(memory_space=pl.ANY)
     vmem = pl.BlockSpec(memory_space=pltpu.VMEM)
-    sems = 6 * Reducer.SEMS + 24 + 12
+    sems = 6 * Reducer.SEMS + 2 + 12
     rows = [pltpu.VMEM((4, 2, 4, 2, 16, 512), BF), pltpu.VMEM((TAIL, 512), BF)]
     return pl.pallas_call(
         finish_kernel,
@@ -1613,7 +1688,7 @@
         in_specs=[any_] * 13 + [vmem] * 6,
         out_specs=(vmem,) * 4,
         scratch_shapes=[
-            pltpu.VMEM((HEADS, 256, WIDE), BF),
+            pltpu.VMEM((HEADS, WIRE, 256), BF),
             pltpu.VMEM((LEAD, QKV), BF),
             pltpu.VMEM((256, QKV), BF),
             pltpu.VMEM((512, QKV), BF),
@@ -1633,7 +1708,7 @@
         + [
             pltpu.SemaphoreType.DMA((sems,)),
             pltpu.SemaphoreType.DMA((sems,)),
-            pltpu.SemaphoreType.DMA((2,)),
+            pltpu.SemaphoreType.DMA((13,)),
         ],
         compiler_params=mesh_params(tag),
         name="finish",
@@ -1814,7 +1889,7 @@
         jnp.concatenate([up[:, FIRST:], down[:, FIRST:]], axis=1), SECOND_CHUNK, SECOND_TOTAL
     )
     lines = (ln1_gain, ln1_bias, ln2_gain, ln2_bias, b_out, b_fc2, b_query, b_value)
-    x, g, h_main, h_tail, attn_tail, out_tail, vec, packed, keep, o, attn, first = front(
+    x, g, attn_tail, out_tail, vec, packed, keep, o, attn, first, h_main, h_tail = front(
         attn_slab,
         first_slab,
         tokens.reshape(256, D),
@@ -1824,7 +1899,7 @@
         0,
     )
     attn = attn.reshape(LEAD, ATTN_TOTAL)
-    (mixed, go, dmid, dy, gvec2, gbias1, dpre, active), o_turned, h_turned, g_turned = middle(
+    (mixed, go, dmid, gvec2, gbias1, dy, dpre, active), o_turned, h_turned, g_turned = middle(
         attn, first, second_slab, o, x, g, out_tail, vec, b_fc1, 2
     )
     first_share, dheads = attend_back_reduce(

time: 316 us -> 293 us (0.927)
  Pallas kernels: 306 us -> 283 us
    pallas_call x1, Pallas kernels: 80.3 us -> 70.5 us  [attend_back_reduce(): pl.pallas_call(back_kernel, out_shape=(jax.ShapeDtypeStruct((16, FIRST_TO...]
    pallas_call x1, Pallas kernels: 109 us -> 100 us  [front(): pl.pallas_call(front_kernel, out_shape=(jax.ShapeDtypeStruct((256, D), BF...]
    pallas_call x1, Pallas kernels: 64.5 us -> 60.7 us  [finish(): pl.pallas_call(finish_kernel, out_shape=(jax.ShapeDtypeStruct((256, D), B...]
where the time goes in v2:
time: 293 us; the launch traced here: 290 us
  Pallas kernels  283 us (97%)
    pallas_call x1, Pallas kernels, front(): pl.pallas_call(front_kernel, out_shape=(jax.ShapeDtypeStruct((256, D), BF...  100 us
    pallas_call x1, Pallas kernels, attend_back_reduce(): pl.pallas_call(back_kernel, out_shape=(jax.ShapeDtypeStruct((16, FIRST_TO...  70.5 us
    pallas_call x1, Pallas kernels, finish(): pl.pallas_call(finish_kernel, out_shape=(jax.ShapeDtypeStruct((256, D), B...  60.7 us
    pallas_call x1, Pallas kernels, middle(): pl.pallas_call(middle_kernel, out_shape=tuple([jax.ShapeDtypeStruct((256,...  44.9 us
    pallas_call x1, Pallas kernels, close_layer(): pl.pallas_call(close_kernel, out_shape=(jax.ShapeDtypeStruct((256, D), BF...  6.08 us

profile of v2, /device:TPU:0, one launch (start us, length us, event | category | flops | bytes accessed | tf_op | source)
XLA Modules:
  0.0 289.7 jit_solution(4085720061805801964)
XLA Ops:
  0.7 0.0 copy-start
  0.7 0.8 copy-done
  1.5 0.0 copy-start.1
  1.5 0.0 copy-start.2
  1.5 0.5 fusion.5
  2.0 0.5 copy-done.1
  2.4 0.1 copy-done.2
  2.5 0.0 copy-start.3
  2.5 0.0 copy-start.4
  2.5 0.0 copy-start.5
  2.6 0.7 pad_maximum_fusion.3.slab
  3.4 0.7 pad_maximum_fusion.1.first_slab
  4.1 0.0 copy-done.3
  4.1 0.3 reshape.83
  4.3 0.0 copy-done.4
  4.4 0.3 reshape.82
  4.6 0.0 copy-done.5
  4.6 0.3 reshape.84
  4.9 0.6 pad_maximum_fusion
  5.5 0.4 reshape.73
  6.0 0.7 pad_maximum_fusion.2.slab
  6.7 100.5 %front.1 = (bf16[256,1152]{1,0:T(8,128)(2,1)}, bf16[256,1152]{1,0:T(8,128)(2,1)}, bf16[128,3456]{1,0:T(8,128)(2,1)}, bf16[128,1152]{1,0:T(8,128)(2,1)}, f32[8,11...) custom-call(bf16[16,5376]{1,0:T(8,128)(2,1)} %pad_maximum_fusion.2.s, ...), custom_call_target="tpu_custom_call" | custom-call | tf_op jit(solution)/shard_map/front/pallas_call | solution.py:1193
  107.2 44.9 %middle.1 = (bf16[256,1152]{1,0:T(8,128)(2,1)}, bf16[16,80,256]{2,1,0:T(8,128)(2,1)}, f32[256,1152]{1,0:T(8,128)}, f32[8,1152]{1,0:T(8,128)}, f32[1,4352]{1,0:T(...) custom-call(bf16[1024,5376]{1,0:T(8,128)(2,1)} %bitcast.10, ...), custom_call_target="tpu_custom_call" | custom-call | tf_op jit(solution)/shard_map/middle/pallas_call | solution.py:1432
  152.1 70.5 %attend_back_reduce.1 = (bf16[16,6912]{1,0:T(8,128)(2,1)}, bf16[16,224,256]{2,1,0:T(8,128)(2,1)}) custom-call(bf16[16,80,256]{2,1,0:T(8,128)(2,1)} %get-tuple-element.73.go, bf16[512,4352]{1,0:T(8,128)(2,1)} %get-tuple-element.74.dpre, bf16[512,4352]{1,0:T(8,128)(2,1)} %get-tuple-element.75.active, ...), custom_call_target="tpu_custom_call" | custom-call | tf_op jit(solution)/shard_map/attend_back_reduce/pallas_call | solution.py:894
  222.6 60.7 %finish.1 = (bf16[256,1152]{1,0:T(8,128)(2,1)}, f32[16,1152]{1,0:T(8,128)}, bf16[16,5376]{1,0:T(8,128)(2,1)}, bf16[16,3072]{1,0:T(8,128)(2,1)}) custom-call(bf16[16,224,256]{2,1,0:T(8,128)(2,1)} %get-tuple-element.82.dheads, bf16[1024,5376]{1,0:T(8,128)(2,1)} %bitcast.11, bf16[512,1152]{1,0:T(8,128)(2,1)} %get-tuple-element.83.dy, ...), custom_call_target="tpu_custom_call" | custom-call | tf_op jit(solution)/shard_map/finish/pallas_call | solution.py:1680
  283.3 6.1 %close_layer.1 = (bf16[256,1152]{1,0:T(8,128)(2,1)}, bf16[256,1152]{1,0:T(8,128)(2,1)}, f32[18,1152]{1,0:T(8,128)}, f32[18,1152]{1,0:T(8,128)}, f32[18,1152]{1,0...) custom-call(f32[16,1152]{1,0:T(8,128)} %get-tuple-element.92.totals_, ...), custom_call_target="tpu_custom_call" | custom-call | tf_op jit(solution)/shard_map/close_layer/pallas_call | solution.py:1812
  (15 shorter events, 0.2 us)
Async XLA Ops:
  0.7 0.8 copy-start
  1.5 0.9 copy-start.1
  1.5 1.0 copy-start.2
  2.5 1.6 copy-start.3
  2.5 1.8 copy-start.4
  2.5 2.1 copy-start.5

commit v3 on v2

--- a/solution.py
+++ b/solution.py
@@ -566,7 +566,7 @@
 FIRST = 3072
 FIRST_CHUNK = 768
 FIRST_TOTAL = 6912
-FIRST_WIDTHS = (1152, 1152, 1152)
+FIRST_WIDTHS = (896, 1408, 1152)
 FIRST_STEP = 768
 SECOND = FF_PAD - FIRST
 SECOND_CHUNK = 384
@@ -786,8 +786,6 @@
     for copy in loads:
         copy.wait()
     maker.run()
-    for spot in range(4):
-        red.pass_on(spot)
     ins[0].finish(0)
 
     def block(step, carry):
@@ -868,6 +866,11 @@
             wire[:, lanes(row * ROW, ROW)] = jnp.transpose(whole)[:WIRE]
             for micro in range(2):
                 pl.when(row == micro)(functools.partial(outs[micro].start, micro))
+
+        @pl.when(step == 1)
+        def _():
+            for spot in range(4):
+                red.pass_on(spot)
 
         @pl.when(step >= 4)
         def _():
@@ -967,25 +970,45 @@
     return [swapper.device(swapper.member(k)) for k in range(1, 16) if k not in (1, 4, 8, 12)]
 
 
+def pack_rows(sources, width, chunk, slab, rest, block):
+    slab[...] = jnp.zeros_like(slab)
+    rest[...] = jnp.zeros_like(rest)
+    for index, (ref, start, stop) in enumerate(sources):
+        place = slice(index * width, index * width + stop - start)
+        slab[:, place] = ref[0:16, start:stop]
+        rest[:, place] = ref[16:18, start:stop].astype(F32)
+    main = len(sources) * width
+    for row in range(2):
+        for index in range(8):
+            spot = row * 8 + index
+            block[spot : spot + 1, :chunk] = rest[
+                row : row + 1, index * chunk : (index + 1) * chunk
+            ]
+    slab[:, main : main + chunk] = block[:, :chunk].astype(BF)
+
+
 def front_kernel(
     slab,
-    first_slab,
     picture,
     tokens_ref,
     cotangent_ref,
+    up_ref,
+    down_ref,
     *refs,
 ):
     lines, rest = refs[:8], refs[8:]
-    run_front(slab, first_slab, picture, tokens_ref, cotangent_ref, lines, *rest)
+    run_front(slab, picture, tokens_ref, cotangent_ref, up_ref, down_ref, lines, *rest)
 
 
 def run_front(
     slab,
-    first_slab,
     picture,
     tokens_ref,
     cotangent_ref,
+    up_ref,
+    down_ref,
     lines,
+    second_slab,
     x_ref,
     g_ref,
     tail_ref,
@@ -998,6 +1021,9 @@
     first_out,
     h_main_all,
     h_tail_all,
+    first_slab,
+    rest,
+    rest_block,
     h_main,
     h_tail,
     full,
@@ -1031,6 +1057,14 @@
     twin = Twin(place, core, send, recv, base + 32)
     greet(line_peers(place, core) + swap_only(ins[0]))
     red.start()
+    pack_rows(
+        [(up_ref, 0, FIRST), (down_ref, 0, FIRST)],
+        FIRST,
+        FIRST_CHUNK,
+        first_slab,
+        rest,
+        rest_block,
+    )
     first.start()
     ids_in = fetch_ids(picture, found, local.at[0])
     ids_in.start()
@@ -1050,6 +1084,14 @@
     lax.fori_loop(0, 3, mix, 0)
     red.second()
     lax.fori_loop(3, 9, mix, 0)
+    pack_rows(
+        [(up_ref, FIRST, FF), (down_ref, FIRST, FF)],
+        SECOND,
+        SECOND_CHUNK,
+        second_slab,
+        rest,
+        rest_block,
+    )
     unit, _ = normal(x_ref[...].astype(F32))
     low[...] = (unit * mixed_vec_ref[0:1] + mixed_vec_ref[1:2]).astype(BF)
     for steps in (1, 2, 3):
@@ -1185,7 +1227,7 @@
     twin.drain()
 
 
-def front(slab, first_slab, tokens, cotangent, lines, picture, tag):
+def front(slab, up, down, tokens, cotangent, lines, picture, tag):
     any_ = pl.BlockSpec(memory_space=pl.ANY)
     vmem = pl.BlockSpec(memory_space=pltpu.VMEM)
     sems = 2 * (3 * Gatherer.SEMS + 3) + 64 + 4
@@ -1193,6 +1235,7 @@
     return pl.pallas_call(
         front_kernel,
         out_shape=(
+            jax.ShapeDtypeStruct((16, SECOND_TOTAL), BF),
             jax.ShapeDtypeStruct((256, D), BF),
             jax.ShapeDtypeStruct((256, D), BF),
             jax.ShapeDtypeStruct((TAIL, QKV), BF),
@@ -1206,9 +1249,12 @@
             jax.ShapeDtypeStruct((4, 2, 4, 2, 16, 512), BF),
             jax.ShapeDtypeStruct((TAIL, 512), BF),
         ),
-        in_specs=[any_] * 3 + [vmem] * 10,
-        out_specs=(vmem,) * 7 + (any_,) * 5,
+        in_specs=[any_] * 2 + [vmem] * 12,
+        out_specs=(vmem,) * 8 + (any_,) * 5,
         scratch_shapes=[
+            pltpu.VMEM((16, FIRST_TOTAL), BF),
+            pltpu.VMEM((2, 8 * FIRST_CHUNK), F32),
+            pltpu.VMEM((16, FIRST_CHUNK), F32),
             pltpu.VMEM((4, 2, 4, 2, 16, 256), BF),
             pltpu.VMEM((TAIL, 256), BF),
             pltpu.VMEM(full, BF),
@@ -1233,7 +1279,7 @@
         ],
         compiler_params=mesh_params(tag),
         name="front",
-    )(slab, first_slab, picture, tokens, cotangent, *lines)
+    )(slab, picture, tokens, cotangent, up, down, *lines)
 
 
 def middle_kernel(
@@ -1488,7 +1534,7 @@
             targets = [
                 (over, device_at(moved(self.place, axis, over), self.core)) for over in (2, 1, 3)
             ]
-        self.slots[stage, spot] = value
+        self.slots[stage, spot] = value.astype(BF)
         for over, device in targets:
             index = self.base + stage * 3 + over - 1
             slot = self.slots.at[stage, spot]
@@ -1503,9 +1549,9 @@
             remote(
                 slot, slot, self.send.at[index], self.recv.at[index], device_at(self.place, self.core)
             ).wait_recv()
-        total = self.slots[stage, 0]
+        total = self.slots[stage, 0].astype(F32)
         for spot in range(1, count):
-            total = total + self.slots[stage, spot]
+            total = total + self.slots[stage, spot].astype(F32)
         return total
 
     def drain(self):
@@ -1701,7 +1747,7 @@
             pltpu.VMEM((ATTN_CHUNK // LANES, LEAD, LANES), F32),
             pltpu.VMEM((D, 256), F32),
             pltpu.VMEM((VEC_ROWS, D), F32),
-            pltpu.VMEM((4, 4, VEC_ROWS, D), F32),
+            pltpu.VMEM((4, 4, VEC_ROWS, D), BF),
         ]
         + Reducer.scratch(ATTN_WIDTHS)
         + Reducer.scratch(SECOND_WIDTHS)
@@ -1880,18 +1926,11 @@
         ATTN_CHUNK,
         ATTN_TOTAL,
     )
-    gap = ((0, 0), (0, FF_PAD - FF))
-    up, down = jnp.pad(w_fc1, gap), jnp.pad(w_fc2.T, gap)
-    first_slab = pack_slab(
-        jnp.concatenate([up[:, :FIRST], down[:, :FIRST]], axis=1), FIRST_CHUNK, FIRST_TOTAL
-    )
-    second_slab = pack_slab(
-        jnp.concatenate([up[:, FIRST:], down[:, FIRST:]], axis=1), SECOND_CHUNK, SECOND_TOTAL
-    )
     lines = (ln1_gain, ln1_bias, ln2_gain, ln2_bias, b_out, b_fc2, b_query, b_value)
-    x, g, attn_tail, out_tail, vec, packed, keep, o, attn, first, h_main, h_tail = front(
+    second_slab, x, g, attn_tail, out_tail, vec, packed, keep, o, attn, first, h_main, h_tail = front(
         attn_slab,
-        first_slab,
+        w_fc1,
+        w_fc2.T,
         tokens.reshape(256, D),
         cotangent.reshape(256, D),
         lines,

time: 293 us -> 288 us (0.983)
  Pallas kernels: 283 us -> 280 us
where the time goes in v3:
time: 288 us; the launch traced here: 285 us
  Pallas kernels  280 us (97%)
    pallas_call x1, Pallas kernels, front(): pl.pallas_call(front_kernel, out_shape=(jax.ShapeDtypeStruct((16, SECOND_...  100 us
    pallas_call x1, Pallas kernels, attend_back_reduce(): pl.pallas_call(back_kernel, out_shape=(jax.ShapeDtypeStruct((16, FIRST_TO...  69.6 us
    pallas_call x1, Pallas kernels, finish(): pl.pallas_call(finish_kernel, out_shape=(jax.ShapeDtypeStruct((256, D), B...  59.7 us
    pallas_call x1, Pallas kernels, middle(): pl.pallas_call(middle_kernel, out_shape=tuple([jax.ShapeDtypeStruct((256,...  44.6 us
    pallas_call x1, Pallas kernels, close_layer(): pl.pallas_call(close_kernel, out_shape=(jax.ShapeDtypeStruct((256, D), BF...  6.08 us

profile of v3, /device:TPU:0, one launch (start us, length us, event | category | flops | bytes accessed | tf_op | source)
XLA Modules:
  0.0 285.2 jit_solution(24859509510345481)
XLA Ops:
  0.7 0.0 copy-start
  0.7 0.8 copy-done
  1.5 0.0 copy-start.1
  1.5 0.0 copy-start.2
  1.5 0.0 copy-start.3
  1.5 0.5 fusion.5
  2.0 0.3 copy-done.1
  2.3 0.3 reshape.75
  2.6 0.0 copy-done.2
  2.6 0.3 reshape.74
  2.9 0.0 copy-done.3
  2.9 0.3 reshape.76
  3.1 0.6 pad_maximum_fusion
  3.8 0.4 reshape.67
  4.2 0.7 maximum_maximum_fusion.slab
  4.9 100.0 %front.1 = (bf16[16,3072]{1,0:T(8,128)(2,1)}, bf16[256,1152]{1,0:T(8,128)(2,1)}, bf16[256,1152]{1,0:T(8,128)(2,1)}, bf16[128,3456]{1,0:T(8,128)(2,1)}, bf16[128,...) custom-call(bf16[16,5376]{1,0:T(8,128)(2,1)} %maximum_maximum_fusion, ...), custom_call_target="tpu_custom_call" | custom-call | tf_op jit(solution)/shard_map/front/pallas_call | solution.py:1235
  104.9 44.6 %middle.1 = (bf16[256,1152]{1,0:T(8,128)(2,1)}, bf16[16,80,256]{2,1,0:T(8,128)(2,1)}, f32[256,1152]{1,0:T(8,128)}, f32[8,1152]{1,0:T(8,128)}, f32[1,4352]{1,0:T(...) custom-call(bf16[1024,5376]{1,0:T(8,128)(2,1)} %bitcast.10, ...), custom_call_target="tpu_custom_call" | custom-call | tf_op jit(solution)/shard_map/middle/pallas_call | solution.py:1478
  149.5 69.6 %attend_back_reduce.1 = (bf16[16,6912]{1,0:T(8,128)(2,1)}, bf16[16,224,256]{2,1,0:T(8,128)(2,1)}) custom-call(bf16[16,80,256]{2,1,0:T(8,128)(2,1)} %get-tuple-element.75.go, bf16[512,4352]{1,0:T(8,128)(2,1)} %get-tuple-element.76.dpre, bf16[512,4352]{1,0:T(8,128)(2,1)} %get-tuple-element.77.active, ...), custom_call_target="tpu_custom_call" | custom-call | tf_op jit(solution)/shard_map/attend_back_reduce/pallas_call | solution.py:897
  219.1 59.7 %finish.1 = (bf16[256,1152]{1,0:T(8,128)(2,1)}, f32[16,1152]{1,0:T(8,128)}, bf16[16,5376]{1,0:T(8,128)(2,1)}, bf16[16,3072]{1,0:T(8,128)(2,1)}) custom-call(bf16[16,224,256]{2,1,0:T(8,128)(2,1)} %get-tuple-element.84.dheads, bf16[1024,5376]{1,0:T(8,128)(2,1)} %bitcast.11, bf16[512,1152]{1,0:T(8,128)(2,1)} %get-tuple-element.85.dy, ...), custom_call_target="tpu_custom_call" | custom-call | tf_op jit(solution)/shard_map/finish/pallas_call | solution.py:1726
  278.8 6.1 %close_layer.1 = (bf16[256,1152]{1,0:T(8,128)(2,1)}, bf16[256,1152]{1,0:T(8,128)(2,1)}, f32[18,1152]{1,0:T(8,128)}, f32[18,1152]{1,0:T(8,128)}, f32[18,1152]{1,0...) custom-call(f32[16,1152]{1,0:T(8,128)} %get-tuple-element.94.totals_, ...), custom_call_target="tpu_custom_call" | custom-call | tf_op jit(solution)/shard_map/close_layer/pallas_call | solution.py:1858
  (7 shorter events, 0.1 us)
Async XLA Ops:
  0.7 0.8 copy-start
  1.5 0.8 copy-start.1
  1.5 1.1 copy-start.2
  1.5 1.4 copy-start.3

commit v4 on v3

--- a/solution.py
+++ b/solution.py
@@ -1380,8 +1380,6 @@
         return read
 
     spread_tail(tile_of(weights, 2 * FIRST), FIRST_CHUNK, wide, tail)
-    red.fourth(0)
-    red.fourth(1)
 
     def deliver(number, place_all):
         for item, (source, target) in enumerate(((dpre_ref, dpre_all), (active_ref, active_all))):
@@ -1419,10 +1417,10 @@
 
         @pl.when(index == 0)
         def _():
-            red.fourth(2)
-            red.fourth(3)
-
-        @pl.when(index == 1)
+            for steps in range(4):
+                red.fourth(steps)
+
+        @pl.when(index == 2)
         def _():
             for steps in range(4):
                 red.fifth(steps)

time: 288 us -> 285 us (0.990)
  Pallas kernels: 280 us -> 277 us
where the time goes in v4:
time: 285 us; the launch traced here: 282 us
  Pallas kernels  277 us (97%)
    pallas_call x1, Pallas kernels, front(): pl.pallas_call(front_kernel, out_shape=(jax.ShapeDtypeStruct((16, SECOND_...  100 us
    pallas_call x1, Pallas kernels, attend_back_reduce(): pl.pallas_call(back_kernel, out_shape=(jax.ShapeDtypeStruct((16, FIRST_TO...  69.1 us
    pallas_call x1, Pallas kernels, finish(): pl.pallas_call(finish_kernel, out_shape=(jax.ShapeDtypeStruct((256, D), B...  58.5 us
    pallas_call x1, Pallas kernels, middle(): pl.pallas_call(middle_kernel, out_shape=tuple([jax.ShapeDtypeStruct((256,...  42.9 us
    pallas_call x1, Pallas kernels, close_layer(): pl.pallas_call(close_kernel, out_shape=(jax.ShapeDtypeStruct((256, D), BF...  6.08 us

profile of v4, /device:TPU:0, one launch (start us, length us, event | category | flops | bytes accessed | tf_op | source)
XLA Modules:
  0.0 281.8 jit_solution(5332776516052542787)
XLA Ops:
  0.7 0.0 copy-start
  0.7 0.8 copy-done
  1.5 0.0 copy-start.1
  1.5 0.0 copy-start.2
  1.5 0.0 copy-start.3
  1.5 0.5 fusion.5
  2.0 0.3 copy-done.1
  2.3 0.3 reshape.75
  2.6 0.0 copy-done.2
  2.6 0.3 reshape.74
  2.9 0.0 copy-done.3
  2.9 0.3 reshape.76
  3.1 0.6 pad_maximum_fusion
  3.8 0.4 reshape.67
  4.2 0.7 maximum_maximum_fusion.slab
  4.9 100.0 %front.1 = (bf16[16,3072]{1,0:T(8,128)(2,1)}, bf16[256,1152]{1,0:T(8,128)(2,1)}, bf16[256,1152]{1,0:T(8,128)(2,1)}, bf16[128,3456]{1,0:T(8,128)(2,1)}, bf16[128,...) custom-call(bf16[16,5376]{1,0:T(8,128)(2,1)} %maximum_maximum_fusion, ...), custom_call_target="tpu_custom_call" | custom-call | tf_op jit(solution)/shard_map/front/pallas_call | solution.py:1235
  104.9 42.9 %middle.1 = (bf16[256,1152]{1,0:T(8,128)(2,1)}, bf16[16,80,256]{2,1,0:T(8,128)(2,1)}, f32[256,1152]{1,0:T(8,128)}, f32[8,1152]{1,0:T(8,128)}, f32[1,4352]{1,0:T(...) custom-call(bf16[1024,5376]{1,0:T(8,128)(2,1)} %bitcast.10, ...), custom_call_target="tpu_custom_call" | custom-call | tf_op jit(solution)/shard_map/middle/pallas_call | solution.py:1476
  147.8 69.1 %attend_back_reduce.1 = (bf16[16,6912]{1,0:T(8,128)(2,1)}, bf16[16,224,256]{2,1,0:T(8,128)(2,1)}) custom-call(bf16[16,80,256]{2,1,0:T(8,128)(2,1)} %get-tuple-element.75.go, bf16[512,4352]{1,0:T(8,128)(2,1)} %get-tuple-element.76.dpre, bf16[512,4352]{1,0:T(8,128)(2,1)} %get-tuple-element.77.active, ...), custom_call_target="tpu_custom_call" | custom-call | tf_op jit(solution)/shard_map/attend_back_reduce/pallas_call | solution.py:897
  216.9 58.5 %finish.1 = (bf16[256,1152]{1,0:T(8,128)(2,1)}, f32[16,1152]{1,0:T(8,128)}, bf16[16,5376]{1,0:T(8,128)(2,1)}, bf16[16,3072]{1,0:T(8,128)(2,1)}) custom-call(bf16[16,224,256]{2,1,0:T(8,128)(2,1)} %get-tuple-element.84.dheads, bf16[1024,5376]{1,0:T(8,128)(2,1)} %bitcast.11, bf16[512,1152]{1,0:T(8,128)(2,1)} %get-tuple-element.85.dy, ...), custom_call_target="tpu_custom_call" | custom-call | tf_op jit(solution)/shard_map/finish/pallas_call | solution.py:1724
  275.4 6.1 %close_layer.1 = (bf16[256,1152]{1,0:T(8,128)(2,1)}, bf16[256,1152]{1,0:T(8,128)(2,1)}, f32[18,1152]{1,0:T(8,128)}, f32[18,1152]{1,0:T(8,128)}, f32[18,1152]{1,0...) custom-call(f32[16,1152]{1,0:T(8,128)} %get-tuple-element.94.totals_, ...), custom_call_target="tpu_custom_call" | custom-call | tf_op jit(solution)/shard_map/close_layer/pallas_call | solution.py:1856
  (7 shorter events, 0.1 us)
Async XLA Ops:
  0.7 0.8 copy-start
  1.5 0.8 copy-start.1
  1.5 1.1 copy-start.2
  1.5 1.4 copy-start.3

commit v5 on v4

--- a/solution.py
+++ b/solution.py
@@ -257,16 +257,16 @@
         size = ref.shape[0] // 2
         return ref.at[pl.ds(half * size, size)]
 
-    def far_out(self):
+    def far_out(self, part):
+        three = ORDERS[part][2]
         for spot in range(4):
-            for part, (one, two, three) in enumerate(ORDERS):
-                for half, way in ((0, 3), (1, 1)):
-                    self.push(
-                        self.half_of(self.acc[part].at[2, spot], half),
-                        self.mid[part].at[half, spot],
-                        self.slot(part, "mid", half * 4 + spot),
-                        device_at(moved(self.place, three, way), self.core),
-                    )
+            for half, way in ((0, 3), (1, 1)):
+                self.push(
+                    self.half_of(self.acc[part].at[2, spot], half),
+                    self.mid[part].at[half, spot],
+                    self.slot(part, "mid", half * 4 + spot),
+                    device_at(moved(self.place, three, way), self.core),
+                )
 
     def pass_on(self, spot):
         for part, (one, two, three) in enumerate(ORDERS):
@@ -455,7 +455,7 @@
         self.pack_tail()
         for part in range(3):
             self.make(part)
-        self.red.far_out()
+            self.red.far_out(part)
 
 
 SWAP_ORDER = (9, 11, 5, 13, 7, 15, 1, 3, 8, 10, 4, 12, 6, 14, 2)

time: 285 us -> 285 us (level)
  no operation moved by 1% of the time
where the time goes in v5:
time: 285 us; the launch traced here: 282 us
  Pallas kernels  277 us (97%)
    pallas_call x1, Pallas kernels, front(): pl.pallas_call(front_kernel, out_shape=(jax.ShapeDtypeStruct((16, SECOND_...  100 us
    pallas_call x1, Pallas kernels, attend_back_reduce(): pl.pallas_call(back_kernel, out_shape=(jax.ShapeDtypeStruct((16, FIRST_TO...  69 us
    pallas_call x1, Pallas kernels, finish(): pl.pallas_call(finish_kernel, out_shape=(jax.ShapeDtypeStruct((256, D), B...  59.3 us
    pallas_call x1, Pallas kernels, middle(): pl.pallas_call(middle_kernel, out_shape=tuple([jax.ShapeDtypeStruct((256,...  42.9 us
    pallas_call x1, Pallas kernels, close_layer(): pl.pallas_call(close_kernel, out_shape=(jax.ShapeDtypeStruct((256, D), BF...  6.08 us

profile of v5, /device:TPU:0, one launch (start us, length us, event | category | flops | bytes accessed | tf_op | source)
XLA Modules:
  0.0 282.4 jit_solution(16071159003674061041)
XLA Ops:
  0.7 0.0 copy-start
  0.7 0.8 copy-done
  1.5 0.0 copy-start.1
  1.5 0.0 copy-start.2
  1.5 0.0 copy-start.3
  1.5 0.5 fusion.5
  2.0 0.3 copy-done.1
  2.3 0.3 reshape.75
  2.6 0.0 copy-done.2
  2.6 0.3 reshape.74
  2.9 0.0 copy-done.3
  2.9 0.3 reshape.76
  3.1 0.6 pad_maximum_fusion
  3.8 0.4 reshape.67
  4.2 0.7 maximum_maximum_fusion.slab
  4.9 100.0 %front.1 = (bf16[16,3072]{1,0:T(8,128)(2,1)}, bf16[256,1152]{1,0:T(8,128)(2,1)}, bf16[256,1152]{1,0:T(8,128)(2,1)}, bf16[128,3456]{1,0:T(8,128)(2,1)}, bf16[128,...) custom-call(bf16[16,5376]{1,0:T(8,128)(2,1)} %maximum_maximum_fusion, ...), custom_call_target="tpu_custom_call" | custom-call | tf_op jit(solution)/shard_map/front/pallas_call | solution.py:1235
  104.9 42.9 %middle.1 = (bf16[256,1152]{1,0:T(8,128)(2,1)}, bf16[16,80,256]{2,1,0:T(8,128)(2,1)}, f32[256,1152]{1,0:T(8,128)}, f32[8,1152]{1,0:T(8,128)}, f32[1,4352]{1,0:T(...) custom-call(bf16[1024,5376]{1,0:T(8,128)(2,1)} %bitcast.10, ...), custom_call_target="tpu_custom_call" | custom-call | tf_op jit(solution)/shard_map/middle/pallas_call | solution.py:1476
  147.8 69.0 %attend_back_reduce.1 = (bf16[16,6912]{1,0:T(8,128)(2,1)}, bf16[16,224,256]{2,1,0:T(8,128)(2,1)}) custom-call(bf16[16,80,256]{2,1,0:T(8,128)(2,1)} %get-tuple-element.75.go, bf16[512,4352]{1,0:T(8,128)(2,1)} %get-tuple-element.76.dpre, bf16[512,4352]{1,0:T(8,128)(2,1)} %get-tuple-element.77.active, ...), custom_call_target="tpu_custom_call" | custom-call | tf_op jit(solution)/shard_map/attend_back_reduce/pallas_call | solution.py:897
  216.7 59.3 %finish.1 = (bf16[256,1152]{1,0:T(8,128)(2,1)}, f32[16,1152]{1,0:T(8,128)}, bf16[16,5376]{1,0:T(8,128)(2,1)}, bf16[16,3072]{1,0:T(8,128)(2,1)}) custom-call(bf16[16,224,256]{2,1,0:T(8,128)(2,1)} %get-tuple-element.84.dheads, bf16[1024,5376]{1,0:T(8,128)(2,1)} %bitcast.11, bf16[512,1152]{1,0:T(8,128)(2,1)} %get-tuple-element.85.dy, ...), custom_call_target="tpu_custom_call" | custom-call | tf_op jit(solution)/shard_map/finish/pallas_call | solution.py:1724
  276.0 6.1 %close_layer.1 = (bf16[256,1152]{1,0:T(8,128)(2,1)}, bf16[256,1152]{1,0:T(8,128)(2,1)}, f32[18,1152]{1,0:T(8,128)}, f32[18,1152]{1,0:T(8,128)}, f32[18,1152]{1,0...) custom-call(f32[16,1152]{1,0:T(8,128)} %get-tuple-element.94.totals_, ...), custom_call_target="tpu_custom_call" | custom-call | tf_op jit(solution)/shard_map/close_layer/pallas_call | solution.py:1856
  (7 shorter events, 0.1 us)
Async XLA Ops:
  0.7 0.8 copy-start
  1.5 0.8 copy-start.1
  1.5 1.1 copy-start.2
  1.5 1.4 copy-start.3
